TPU v7x, 512 devices: a whole 4x8x8 slice. The times are simulated.
512 devices in a mesh: py: 16 (over x_hi, z), pz: 32 (over y, x_lo, core).
Axes of the slice: x: 4 (x_hi: 2, x_lo: 2; x = x_hi * 2 + x_lo), y: 8, z: 8, core: 2. Of those that a mesh axis runs over, the one named last changes fastest.
Arguments:
- features: bfloat16 [32, 256, 256, 256], P(None, 'py', 'pz'), may hold values from -6 to 6
- spectral_weight: bfloat16 [2, 64, 32, 48, 1024], P(None, 'py', 'pz'), may hold values from -4 to 4
- bypass_weight: bfloat16 [32, 32], replicated, may hold values from -1 to 1
- bias_vector: float32 [32], replicated, may hold values from -3 to 3
Outputs:
- layer_output: bfloat16 [32, 256, 256, 256], P(None, 'py', 'pz')
All inputs are finite; a program needn't handle non-finite values.
Results may differ from a plain program's by a relative error of at most 0.001.
Values sent between devices are 32-bit elements; how exact they have to be, the bound alone decides.
A program may use at most 128 MiB of HBM per device.

v0:
```python
import math

import jax
import jax.numpy as jnp
from jax import lax
from jax.sharding import PartitionSpec as P


def centred(mode_count):
    index_list = jnp.arange(mode_count, dtype=jnp.int32)
    return jnp.where(index_list < mode_count // 2, index_list, index_list - mode_count)


def phases(frequencies, positions, period):
    product = positions[:, None] * frequencies[None, :] % period
    return product.astype(jnp.float32) * jnp.float32(2.0 * math.pi / period)


def forward_pair(frequencies, positions, period):
    angles = phases(frequencies, positions, period)
    cosines = jnp.cos(angles)
    sinewaves = jnp.sin(angles)
    return jnp.stack([jnp.stack([cosines, -sinewaves]), jnp.stack([sinewaves, cosines])])


def inverse_pair(frequencies, positions, period):
    angles = phases(frequencies, positions, period).T
    cosines = jnp.cos(angles)
    sinewaves = jnp.sin(angles)
    return jnp.stack([jnp.stack([cosines, sinewaves]), jnp.stack([-sinewaves, cosines])])


def x_forward_table(mode_count, length, norming):
    angles = phases(
        jnp.arange(mode_count, dtype=jnp.int32), jnp.arange(length, dtype=jnp.int32), length
    )
    table = jnp.stack([jnp.cos(angles) * norming, -jnp.sin(angles) * norming], axis=2)
    return table.reshape(length, 2 * mode_count)


def x_inverse_table(mode_count, length, norming):
    angles = phases(
        jnp.arange(mode_count, dtype=jnp.int32), jnp.arange(length, dtype=jnp.int32), length
    ).T
    factor = jnp.where(jnp.arange(mode_count) == 0, 1.0, 2.0).astype(jnp.float32)[:, None] * norming
    return jnp.stack([jnp.cos(angles) * factor, -jnp.sin(angles) * factor], axis=1)


def per_device(features, spectral_weight, bypass_weight, bias_vector):
    highest = lax.Precision.HIGHEST
    channels, rows_y, rows_z, length = features.shape
    parts_y = lax.axis_size("py")
    parts_z = lax.axis_size("pz")
    full_y = rows_y * parts_y
    full_z = rows_z * parts_z
    kx_local = spectral_weight.shape[1]
    ky_local = spectral_weight.shape[2]
    modes_z = spectral_weight.shape[3]
    modes_x = kx_local * parts_y
    modes_y = ky_local * parts_z
    norming = jnp.float32(1.0 / math.sqrt(length * full_y * full_z))
    flat_rows = features.reshape(channels * rows_y * rows_z, length)
    x_table = x_forward_table(modes_x, length, norming)
    freq_y = centred(modes_y)
    freq_z = centred(modes_z)
    own_y = lax.axis_index("py") * rows_y + jnp.arange(rows_y, dtype=jnp.int32)
    y_own_table = forward_pair(freq_y, own_y, full_y)
    spectrum = jnp.einsum(
        "xa,rx->ar", x_table, flat_rows, precision=highest, preferred_element_type=jnp.float32
    )
    blocks = spectrum.reshape(kx_local * lax.axis_size("py"), 2, channels, rows_y, rows_z)
    summed = lax.psum_scatter(
        jnp.einsum("kpcyz,pqyj->kqcjz", blocks, y_own_table, precision=highest),
        "py",
        scatter_dimension=0,
        tiled=True,
    )
    y_spectrum = summed.reshape(2 * kx_local, channels, modes_y, rows_z)
    z_table = forward_pair(freq_z, jnp.arange(full_z, dtype=jnp.int32), full_z)
    portion = lax.all_to_all(y_spectrum, "pz", split_axis=2, concat_axis=3, tiled=True)
    item_count = portion.shape[1]
    blocks = portion.reshape(kx_local, 2, item_count, ky_local, full_z)
    spectrum = jnp.einsum("kpcaz,pqzm->akqmc", blocks, z_table, precision=highest)
    weights = spectral_weight.astype(jnp.float32).reshape(
        2, kx_local, ky_local, modes_z, channels, channels
    )
    real_in = spectrum[:, :, 0]
    imag_in = spectrum[:, :, 1]

    def contract(values, matrix):
        return jnp.einsum("akmi,kamio->akmo", values, matrix, precision=highest)

    real_out = contract(real_in, weights[0]) - contract(imag_in, weights[1])
    imag_out = contract(imag_in, weights[0]) + contract(real_in, weights[1])
    mixed_modes = jnp.stack([real_out, imag_out], axis=2)
    z_back = inverse_pair(freq_z, jnp.arange(full_z, dtype=jnp.int32), full_z)
    z_inverse = jnp.einsum("akqmo,qrmz->kroaz", mixed_modes, z_back, precision=highest)
    z_inverse = z_inverse.reshape(2 * kx_local, channels, ky_local, full_z)
    returned = lax.all_to_all(z_inverse, "pz", split_axis=3, concat_axis=2, tiled=True)
    x_back_table = x_inverse_table(modes_x, length, norming)
    y_own_back = inverse_pair(freq_y, own_y, full_y)
    per_mode = returned.reshape(kx_local, 2, channels, modes_y, rows_z)
    portion = lax.all_gather(per_mode, "py", axis=0, tiled=True)
    mode_total = portion.shape[0]
    planes = jnp.einsum("kqcjz,qrjy->krcyz", portion, y_own_back, precision=highest)
    all_planes = planes.reshape(mode_total, 2, channels, rows_y * rows_z)
    spectral = jnp.einsum("kqcs,kqx->csx", all_planes, x_back_table, precision=highest)
    flat_field = features.reshape(channels, rows_y * rows_z * length)
    bypass = jnp.einsum("io,ir->or", bypass_weight, flat_field, preferred_element_type=jnp.float32)
    combined = spectral.reshape(channels, rows_y * rows_z * length) + bypass + bias_vector[:, None]
    return jax.nn.gelu(combined).reshape(features.shape).astype(jnp.bfloat16)


def solution(mesh):
    in_specs = (P(None, "py", "pz", None), P(None, "py", "pz", None, None), P(), P())
    out_specs = P(None, "py", "pz", None)
    return jax.shard_map(
        per_device, mesh=mesh, in_specs=in_specs, out_specs=out_specs, check_vma=False
    )
```

profile of v0, /device:TPU:6, one launch (start us, length us, event | category | flops | bytes accessed | tf_op | source)
XLA Modules:
  0.0 669.6 jit_solution(7612353481032413910)
XLA Ops:
  7.3 3.5 fusion.27
  10.8 9.1 %fusion.17 = f32[64,2,32,32,8]{0,3,4,2,1:T(8,128)} fusion(f32[64,2,32,16,8]{0,3,1,4,2:T(8,128)S(1)} %fusion.27, f32[1,2,16,32]{3,2,0,1:T(8,128)S(1)} %get-tuple-element.22, f32[1,2,16,32]{3,2,0,1:T(8,128)S(1)} %get-tuple-element.21), kind=kOutput, calls=%fused_computation.23 | convolution fusion | flops 402655232 | bytes 6299648 | tf_op jit(solution)/shard_map/kpcyz,pqyj->kqcjz/dot_general | solution.py:73
  19.8 16.2 %copy.62 = f32[64,2,32,32,8]{3,4,2,1,0:T(8,128)} copy(f32[64,2,32,32,8]{0,3,4,2,1:T(8,128)} %fusion.17) | data formatting | bytes 8388608 | tf_op jit(solution)/shard_map/kpcyz,pqyj->kqcjz/transpose | solution.py:73
  37.3 294.3 %reduce-scatter.2.cloned.1.call-done = f32[4,2,32,32,8]{3,4,2,1,0:T(8,128)} async-done(((f32[64,2,32,32,8]{3,4,2,1,0:T(8,128)}), f32[4,2,32,32,8]{3,4,2,1,0:T(8,128)}) %reduce-scatter.2.cloned.1.call-update) | async-done | bytes 262160 | tf_op jit(solution)/shard_map/reduce_scatter | solution.py:72
  331.6 2.2 copy.63
  334.9 8.4 %all-to-all-start = ((f32[32,1,2048]{2,1,0:T(1,128)}), f32[32,1,2048]{2,1,0:T(1,128)}, u32[]{:S(2)}, u32[]{:S(2)}) async-start(f32[32,1,2048]{2,1,0:T(1,128)} %reshape.921), calls=%async_computation.1 | async-start | bytes 524288 | tf_op jit(solution)/shard_map/all_to_all | solution.py:80
  344.5 1.2 reshape.888
  345.7 1.2 reshape.890
  346.9 1.6 maximum_bitcast_fusion.10
  349.5 6.0 all-to-all-done
  356.0 2.2 reduce.8
  358.2 1.3 reshape.922
  359.5 1.3 copy.64
  360.8 2.7 convolution_bitcast_fusion.1
  365.0 5.1 fusion.20
  374.5 15.6 %all_to_all.8 = f32[32,1,2048]{2,1,0:T(1,128)S(1)} all-to-all(f32[32,1,2048]{2,1,0:T(1,128)S(1)} %reshape.923), channel_id=1, replica_groups=mesh['py'=16,'pz'=32] {'pz'}, dimensions={0} | all-to-all | bytes 524288 | tf_op jit(solution)/shard_map/all_to_all | solution.py:99
  391.7 1.7 copy.69
  393.4 2.5 copy.118
  396.3 220.9 %all-gather.2.cloned.1.call-done = f32[64,2,32,32,8]{3,4,2,1,0:T(8,128)} async-done(((f32[4,2,32,32,8]{3,4,2,1,0:T(8,128)}), f32[64,2,32,32,8]{3,4,2,1,0:T(8,128)}) %all-gather.2.cloned.1.call-update) | async-done | bytes 4194320 | tf_op jit(solution)/shard_map/all_gather | solution.py:103
  617.3 34.0 %fusion.24 = f32[64,2,32,16,8]{0,3,4,2,1:T(8,128)S(1)} fusion(f32[64,2,32,32,8]{3,4,2,1,0:T(8,128)} %all-gather.2.cloned.1.call-done, f32[1,2,32,16]{2,3,0,1:T(8,128)S(1)} %get-tuple-element.20, f32[1,2,32,16]{2,3,0,1:T(8,128)S(1)} %get-tuple-element.19), kind=kOutput, calls=%fused_computation.28 | convolution fusion | flops 402655232 | bytes 6299648 | tf_op jit(solution)/shard_map/kqcjz,qrjy->krcyz/dot_general | solution.py:105
  651.3 4.4 fusion.12
  655.7 2.4 copy.117
  658.1 2.4 fusion.11
  660.5 1.8 copy.119
  (55 shorter events, 13.5 us)
Async XLA Ops:
  6.5 651.6 %copy-start = (bf16[32,32]{1,0:T(8,128)(2,1)S(1)}, bf16[32,32]{1,0:T(8,128)(2,1)}, u32[]{:S(2)}) copy-start(bf16[32,32]{1,0:T(8,128)(2,1)} %param.6) | copy-start | bytes 6148
  6.5 325.0 %reduce-scatter.2.cloned.1.call-start = ((), (), s32[]{:S(2)}) async-start(), calls=%async_computation.3 | async-start | bytes 17825792 | tf_op jit(solution)/shard_map/reduce_scatter | solution.py:72
  6.8 13.0 %copy-start.5 = (s32[16]{0:T(128)}, s32[16]{0:T(128)S(1)}, u32[]{:S(2)}) copy-start(s32[16]{0:T(128)S(1)} %iota_add_fusion) | copy-start | bytes 196
  36.1 1.1 copy-start.3
  334.9 20.5 %all-to-all-start = ((f32[32,1,2048]{2,1,0:T(1,128)}), f32[32,1,2048]{2,1,0:T(1,128)}, u32[]{:S(2)}, u32[]{:S(2)}) async-start(f32[32,1,2048]{2,1,0:T(1,128)} %reshape.921), calls=%async_computation.1 | async-start | bytes 524288 | tf_op jit(solution)/shard_map/all_to_all | solution.py:80
  343.3 273.9 %all-gather.2.cloned.1.call-start = ((), (), s32[]{:S(2)}) async-start(), calls=%async_computation.4 | async-start | bytes 17825792 | tf_op jit(solution)/shard_map/all_gather | solution.py:103
  359.5 13.7 %copy-start.4 = (f32[1,2,48,256]{3,2,0,1:T(8,128)S(1)}, f32[1,2,48,256]{3,2,0,1:T(8,128)}, u32[]{:S(2)}) copy-start(f32[1,2,48,256]{3,2,0,1:T(8,128)} %get-tuple-element.18) | copy-start | bytes 294916
  373.7 19.7 %copy-start.1 = (bf16[32,16,8,256]{3,2,1,0:T(8,128)(2,1)S(1)}, bf16[32,16,8,256]{3,2,1,0:T(8,128)(2,1)}, u32[]{:S(2)}) copy-start(bf16[32,16,8,256]{3,2,1,0:T(8,128)(2,1)} %param.4) | copy-start | bytes 6291460
  391.3 4.6 copy-start.6
  655.6 2.5 copy-start.2
  655.7 2.5 copy-start.7
Sparse Core Ops, SparseCore 0:
  36.2 295.3 reduce-scatter.1
  393.5 223.7 all-gather.1
where the time goes:
time: 679 us; the launch traced here: 670 us
  waiting for transfers between devices  521 us (77%)
  matrix products  56.4 us (8%)
  local copies, waits for them, and re-layouts  40.7 us (6%)
  blocking collectives  15.6 us (2%)
  between operations  14.2 us (2%)
  other arithmetic  12.8 us (2%)
  starting transfers between devices  8.62 us (1%)
    reduce_scatter x1, waiting for transfers between devices, per_device(): lax.psum_scatter(jnp.einsum('kpcyz,pqyj->kqcjz', blocks, y_own_table, pre...  294 us
    all_gather x1, waiting for transfers between devices, per_device(): portion = lax.all_gather(per_mode, 'py', axis=0, tiled=True)  221 us
    dot_general x1, matrix products, per_device(): jnp.einsum('kqcjz,qrjy->krcyz', portion, y_own_back, precision=highest)  34 us
    transpose x1, local copies, waits for them, and re-layouts, per_device(): jnp.einsum('kpcyz,pqyj->kqcjz', blocks, y_own_table, precision=highest)  16.2 us
    all_to_all x1, blocking collectives, per_device(): lax.all_to_all(z_inverse, 'pz', split_axis=3, concat_axis=2, tiled=True)  15.6 us
  transfers between devices with their start and end apart: 3, of which 3 were waited for; matrix products, arithmetic and copies ran while one was open for 1% of the time, Pallas kernels for 0%

commit v1 on v0

v1 whole, which is shorter than its diff:
```python
import functools
import math

import jax
import jax.numpy as jnp
import ml_dtypes
import numpy as np
from jax import lax
from jax.experimental import pallas as pl
from jax.experimental.pallas import tpu as pltpu
from jax.sharding import PartitionSpec as P

MESH = pl.DeviceIdType.MESH
BF = jnp.bfloat16
F32 = jnp.float32
MIB = 1 << 20


def centred(count):
    index = np.arange(count)
    return np.where(index < count // 2, index, index - count)


def split(table):
    high = table.astype(ml_dtypes.bfloat16)
    low = (table - high.astype(np.float64)).astype(ml_dtypes.bfloat16)
    return high, low


def pair(frequencies, positions, period, sign):
    angle = 2.0 * np.pi * ((positions[:, None] * frequencies[None, :]) % period) / period
    c, s = np.cos(angle), np.sin(angle)
    return np.stack([np.stack([c, sign * s]), np.stack([-sign * s, c])])


def make_tables(nx, ny, nz, mx, my, mz, py, pz):
    k = mx // py
    zl = nz // pz
    yl = ny // py
    norm = 1.0 / math.sqrt(nx * ny * nz)
    angle = 2.0 * np.pi * ((np.arange(mx)[:, None] * np.arange(nx)[None, :]) % nx) / nx
    eye = np.eye(k)
    xf = np.stack([np.cos(angle) * norm, -np.sin(angle) * norm], 1).reshape(2 * mx, nx)
    weight = np.where(np.arange(mx) == 0, 1.0, 2.0)[:, None] * norm
    xi = np.stack([np.cos(angle) * weight, -np.sin(angle) * weight], 1).reshape(2 * mx, nx)
    yf = pair(centred(my), np.arange(ny), ny, -1.0)
    yf = np.einsum("pqyj,kl->jkqylp", yf, eye).reshape(my * k * 2, ny * k * 2)
    yi = pair(centred(my), np.arange(ny), ny, 1.0)
    yi = np.einsum("qryj,kl->ykrjlq", yi, eye).reshape(ny * k * 2, my * k * 2)
    zf = pair(centred(mz), np.arange(nz), nz, -1.0).reshape(2, 2, pz, zl, mz)
    zf = np.einsum("pqszm,kl->zqkmslp", zf, eye).reshape(zl, 2 * k * mz, pz * k * 2)
    zi = pair(centred(mz), np.arange(nz), nz, 1.0).reshape(2, 2, pz, zl, mz)
    zi = np.einsum("qrszm,kl->zskrqlm", zi, eye).reshape(zl, pz * k * 2, 2 * k * mz)
    return xf, xi, yf, yi, zf, zi


def halves(value):
    high = value.astype(BF)
    return high, (value - high.astype(F32)).astype(BF)


def dot(a, b, dims=((1,), (0,))):
    return lax.dot_general(a, b, (dims, ((), ())), preferred_element_type=F32)


def dot3(ah, al, bh, bl):
    return dot(ah, bh) + dot(al, bh) + dot(ah, bl)


def exchange_kernel(axis, n, src, dst, send_sem, recv_sem, own_sem):
    me = lax.axis_index(axis)
    barrier = pltpu.get_barrier_semaphore()

    def greet(step, carry):
        pl.semaphore_signal(
            barrier, inc=1, device_id={axis: lax.rem(me + step, n)}, device_id_type=MESH
        )
        return carry

    lax.fori_loop(1, n, greet, 0)
    pl.semaphore_wait(barrier, n - 1)

    def copy(step):
        peer = lax.rem(me + step, n)
        return pltpu.make_async_remote_copy(
            src_ref=src.at[peer],
            dst_ref=dst.at[me],
            send_sem=send_sem.at[step],
            recv_sem=recv_sem.at[step],
            device_id={axis: peer},
            device_id_type=MESH,
        )

    def start(step, carry):
        copy(step).start()
        return carry

    def finish(step, carry):
        copy(step).wait()
        return carry

    lax.fori_loop(1, n, start, 0)
    own = pltpu.make_async_copy(src.at[me], dst.at[me], own_sem)
    own.start()
    own.wait()
    lax.fori_loop(1, n, finish, 0)


def exchange(blocks, axis, n, ident):
    return pl.pallas_call(
        functools.partial(exchange_kernel, axis, n),
        out_shape=jax.ShapeDtypeStruct(blocks.shape, blocks.dtype),
        in_specs=[pl.BlockSpec(memory_space=pl.ANY)],
        out_specs=pl.BlockSpec(memory_space=pl.ANY),
        scratch_shapes=[
            pltpu.SemaphoreType.DMA((n,)),
            pltpu.SemaphoreType.DMA((n,)),
            pltpu.SemaphoreType.DMA,
        ],
        compiler_params=pltpu.CompilerParams(collective_id=ident, has_side_effects=True),
        name="exchange_" + axis + str(ident),
    )(blocks)


def x_forward_kernel(zl, f_ref, t_ref, o_ref):
    block = f_ref[...].astype(F32)
    channels, rows, length = block.shape
    for y in range(rows // zl):
        field = block[:, y * zl : (y + 1) * zl, :].reshape(channels * zl, length).astype(BF)
        both = dot(t_ref[...], field, ((1,), (1,)))
        half = both.shape[0] // 2
        o_ref[:, y] = (both[:half] + both[half:]).reshape(o_ref.shape[0], o_ref.shape[2], -1)


def y_forward_kernel(x_ref, th_ref, tl_ref, o_ref):
    @pl.when(pl.program_id(0) == 0)
    def _():
        o_ref[...] = jnp.zeros_like(o_ref)

    xh, xl = halves(x_ref[...])
    o_ref[...] += dot3(th_ref[...], tl_ref[...], xh, xl)


def y_inverse_kernel(x_ref, th_ref, tl_ref, o_ref):
    xh, xl = halves(x_ref[...])
    o_ref[...] = dot3(th_ref[...], tl_ref[...], xh, xl)


def middle_kernel(zl, x_ref, w_ref, fh_ref, fl_ref, ih_ref, il_ref, o_ref):
    xh, xl = halves(x_ref[...])
    lanes = x_ref.shape[1]
    channels = lanes // zl
    inner = lax.broadcasted_iota(jnp.int32, (1, lanes), 1) % zl
    modes = jnp.zeros((fh_ref.shape[1], lanes), F32)
    for z in range(zl):
        modes += jnp.where(inner == z, dot3(fh_ref[z], fl_ref[z], xh, xl), 0.0)
    pairs = w_ref.shape[2]
    lane = lax.broadcasted_iota(jnp.int32, (lanes, pairs), 0) // zl
    both = lax.broadcasted_iota(jnp.int32, (lanes, pairs), 1)
    spread = jnp.where(lane == both // channels, 1.0, 0.0).astype(BF)
    mh, ml = halves(modes)
    wide = dot(mh, spread) + dot(ml, spread)
    half = wide.shape[0] // 2
    re, im = wide[:half], wide[half:]
    wr, wi = w_ref[0].astype(F32), w_ref[1].astype(F32)
    mixed = jnp.concatenate([wr * re - wi * im, wr * im + wi * re], axis=0)
    both = lax.broadcasted_iota(jnp.int32, (pairs, lanes), 0)
    lane = lax.broadcasted_iota(jnp.int32, (pairs, lanes), 1) // zl
    gather = jnp.where(both % channels == lane, 1.0, 0.0).astype(BF)
    ph, plo = halves(mixed)
    summed = dot(ph, gather) + dot(plo, gather)
    sh, sl = halves(summed)
    total = jnp.zeros(o_ref.shape, F32)
    for z in range(zl):
        total += jnp.where(inner == z, dot3(ih_ref[z], il_ref[z], sh, sl), 0.0)
    o_ref[...] = total


def x_inverse_kernel(zl, r_ref, f_ref, w_ref, b_ref, th_ref, tl_ref, o_ref, mix_ref, bias_ref):
    channels, rows, length = f_ref.shape
    lanes = channels * zl

    @pl.when(pl.program_id(0) == 0)
    def _():
        row = lax.broadcasted_iota(jnp.int32, (lanes, channels), 0) // zl
        column = lax.broadcasted_iota(jnp.int32, (lanes, channels), 1)
        pick = row == column
        ones = jnp.where(pick, 1.0, 0.0).astype(BF)
        left = dot(ones, w_ref[...], ((1,), (1,))).astype(BF)
        full = dot(left, ones, ((1,), (1,)))
        a = lax.broadcasted_iota(jnp.int32, (lanes, lanes), 0) % zl
        b = lax.broadcasted_iota(jnp.int32, (lanes, lanes), 1) % zl
        mix_ref[...] = jnp.where(a == b, full, 0.0).astype(BF)
        column = jnp.sum(jnp.where(pick, b_ref[...], 0.0), axis=1, keepdims=True)
        bias_ref[...] = jnp.broadcast_to(column, bias_ref.shape)

    block = f_ref[...].astype(F32)
    th, tl, mix, bias = th_ref[...], tl_ref[...], mix_ref[...], bias_ref[...]
    for y in range(rows // zl):
        spectrum = r_ref[:, y].reshape(-1, lanes)
        sh, sl = halves(spectrum)
        field = block[:, y * zl : (y + 1) * zl, :].reshape(lanes, length).astype(BF)
        first = ((0,), (0,))
        value = dot(sh, th, first) + dot(sl, th, first) + dot(sh, tl, first)
        value = value + dot(mix, field) + bias
        out = jax.nn.gelu(value).reshape(channels, zl, length)
        o_ref[:, y * zl : (y + 1) * zl, :] = out.astype(o_ref.dtype)


def params(mib):
    return pltpu.CompilerParams(vmem_limit_bytes=mib * MIB)


def whole(shape):
    return pl.BlockSpec(shape, lambda i: (0,) * len(shape))


def per_device(tables, n_y, n_z, features, spectral_weight, bypass_weight, bias_vector):
    xf, xi, yf, yi, zf, zi = tables
    c, yl, zl, nx = features.shape
    _, kl, _, mz, pairs = spectral_weight.shape
    lanes = c * zl
    part = 2 * kl
    flat = features.reshape(c, yl * zl, nx)
    step = 2
    steps = yl // step

    xh, xl = split(xf)
    x_rows = jnp.asarray(np.concatenate([xh, xl], 0))
    field_spec = pl.BlockSpec((c, step * zl, nx), lambda i: (0, i, 0))
    row_spec = pl.BlockSpec((n_y, step, part, lanes), lambda i: (0, i, 0, 0))
    a = pl.pallas_call(
        functools.partial(x_forward_kernel, zl),
        grid=(steps,),
        in_specs=[field_spec, whole(x_rows.shape)],
        out_specs=row_spec,
        out_shape=jax.ShapeDtypeStruct((n_y, yl, part, lanes), F32),
        compiler_params=params(32),
        name="x_forward",
    )(flat, x_rows)

    a = exchange(a, "py", n_y, 0).reshape(n_y * yl * part, lanes)

    yh, ylo = map(jnp.asarray, split(yf))
    my_rows = yh.shape[0]
    tile = 256
    b = pl.pallas_call(
        y_forward_kernel,
        grid=(a.shape[0] // tile,),
        in_specs=[
            pl.BlockSpec((tile, lanes), lambda i: (i, 0)),
            pl.BlockSpec((my_rows, tile), lambda i: (0, i)),
            pl.BlockSpec((my_rows, tile), lambda i: (0, i)),
        ],
        out_specs=whole((my_rows, lanes)),
        out_shape=jax.ShapeDtypeStruct((my_rows, lanes), F32),
        compiler_params=params(32),
        name="y_forward",
    )(a, yh, ylo)

    b = exchange(b.reshape(n_z, part, lanes), "pz", n_z, 1).reshape(n_z * part, lanes)

    fh, fl = map(jnp.asarray, split(zf))
    ih, il = map(jnp.asarray, split(zi))
    p = pl.pallas_call(
        functools.partial(middle_kernel, zl),
        out_shape=jax.ShapeDtypeStruct((n_z * part, lanes), F32),
        compiler_params=params(48),
        name="middle",
    )(b, spectral_weight.reshape(2, kl * mz, pairs), fh, fl, ih, il)

    p = exchange(p.reshape(n_z, part, lanes), "pz", n_z, 2).reshape(n_z * part, lanes)

    gh, gl = map(jnp.asarray, split(yi))
    q = pl.pallas_call(
        y_inverse_kernel,
        grid=(gh.shape[0] // tile,),
        in_specs=[
            whole(p.shape),
            pl.BlockSpec((tile, gh.shape[1]), lambda i: (i, 0)),
            pl.BlockSpec((tile, gh.shape[1]), lambda i: (i, 0)),
        ],
        out_specs=pl.BlockSpec((tile, lanes), lambda i: (i, 0)),
        out_shape=jax.ShapeDtypeStruct((gh.shape[0], lanes), F32),
        compiler_params=params(32),
        name="y_inverse",
    )(p, gh, gl)

    q = exchange(q.reshape(n_y, yl, part, lanes), "py", n_y, 3)

    th, tl = map(jnp.asarray, split(xi))
    out = pl.pallas_call(
        functools.partial(x_inverse_kernel, zl),
        grid=(steps,),
        in_specs=[
            row_spec,
            field_spec,
            whole(bypass_weight.shape),
            whole((1, c)),
            whole(th.shape),
            whole(tl.shape),
        ],
        out_specs=field_spec,
        out_shape=jax.ShapeDtypeStruct(flat.shape, BF),
        scratch_shapes=[pltpu.VMEM((lanes, lanes), BF), pltpu.VMEM((lanes, nx), F32)],
        compiler_params=params(32),
        name="x_inverse",
    )(q, flat, bypass_weight, bias_vector.reshape(1, c), th, tl)
    return out.reshape(features.shape)


def solution(mesh):
    n_y, n_z = mesh.shape["py"], mesh.shape["pz"]

    def run(features, spectral_weight, bypass_weight, bias_vector):
        _, ny, nz, nx = features.shape
        _, mx, my, mz, _ = spectral_weight.shape
        tables = make_tables(nx, ny, nz, mx, my, mz, n_y, n_z)
        return jax.shard_map(
            functools.partial(per_device, tables, n_y, n_z),
            mesh=mesh,
            in_specs=(P(None, "py", "pz", None), P(None, "py", "pz", None, None), P(), P()),
            out_specs=P(None, "py", "pz", None),
            check_vma=False,
        )(features, spectral_weight, bypass_weight, bias_vector)

    return run
```

time: 679 us -> 187 us (0.28); the launches traced: 670 us -> 185 us
  waiting for transfers between devices: 521 us -> 0 us
  Pallas kernels: 0 us -> 166 us
  matrix products: 56.4 us -> 0 us
  local copies, waits for them, and re-layouts: 40.7 us -> 19 us
  blocking collectives: 15.6 us -> 0 us
  between operations: 14.2 us -> 0.21 us
  other arithmetic: 12.8 us -> 0 us
  starting transfers between devices: 8.62 us -> 0 us
    reduce_scatter x1 -> x0, waiting for transfers between devices: 294 us -> none  [per_device(): lax.psum_scatter(jnp.einsum('kpcyz,pqyj->kqcjz', blocks, y_own_table, pre...]
    all_gather x1 -> x0, waiting for transfers between devices: 221 us -> none  [per_device(): portion = lax.all_gather(per_mode, 'py', axis=0, tiled=True)]
    pallas_call x0 -> x9, Pallas kernels: none -> 166 us  [the longest x4 146 us: exchange(): pl.pallas_call(functools.partial(exchange_kernel, axis, n), out_shape=jax...]
    dot_general x7 -> x0, matrix products: 56.4 us -> none  [the longest x1 34 us: per_device(): jnp.einsum('kqcjz,qrjy->krcyz', portion, y_own_back, precision=highest)]
    transpose x2 -> x0, local copies, waits for them, and re-layouts: 16.3 us -> none  [the longest x1 16.2 us: per_device(): jnp.einsum('kpcyz,pqyj->kqcjz', blocks, y_own_table, precision=highest)]
    all_to_all x1 -> x0, blocking collectives: 15.6 us -> none  [per_device(): lax.all_to_all(z_inverse, 'pz', split_axis=3, concat_axis=2, tiled=True)]
    all_to_all x1 -> x0, starting transfers between devices: 8.4 us -> none  [per_device(): lax.all_to_all(y_spectrum, 'pz', split_axis=2, concat_axis=3, tiled=True)]
    unnamed x25 -> x46, local copies, waits for them, and re-layouts: 12.6 us -> 19 us
  transfers between devices with their start and end apart: 3 -> 0, of which waited for: 3 -> 0; matrix products, arithmetic and copies ran while one was open for 1% -> 0% of each run, Pallas kernels for 0% -> 0%
where the time goes in v1:
time: 187 us; the launch traced here: 185 us
  Pallas kernels  166 us (89%)
  local copies, waits for them, and re-layouts  19 us (10%)
    pallas_call x4, Pallas kernels, exchange(): pl.pallas_call(functools.partial(exchange_kernel, axis, n), out_shape=jax...  146 us
    unnamed x46, local copies, waits for them, and re-layouts  19 us
    pallas_call x1, Pallas kernels, per_device(): pl.pallas_call(functools.partial(middle_kernel, zl), out_shape=jax.ShapeD...  6.32 us
    pallas_call x1, Pallas kernels, per_device(): pl.pallas_call(functools.partial(x_inverse_kernel, zl), grid=(steps,), in...  6.27 us

profile of v1, /device:TPU:6, one launch (start us, length us, event | category | flops | bytes accessed | tf_op | source)
XLA Modules:
  0.0 185.3 jit_solution(2939424965736898587)
XLA Ops:
  0.0 1.6 copy-done
  1.6 0.9 copy-done.18
  2.5 2.4 %x_forward.1.src = f32[16,16,8,256]{3,2,1,0:T(8,128)S(1)} custom-call(bf16[32,128,256]{2,1,0:T(8,128)(2,1)S(1)} %bitcast.10, bf16[256,256]{1,0:T(8,128)(2,1)S(1)} %copy-done.18), custom_call_target="tpu_custom_call" | custom-call | tf_op jit(solution)/shard_map/x_forward/pallas_call | solution.py:232
  5.0 1.3 copy-done.5
  6.3 59.9 %exchange_py0.1 = f32[16,16,8,256]{3,2,1,0:T(8,128)} custom-call(f32[16,16,8,256]{3,2,1,0:T(8,128)} %copy-done.5), custom_call_target="tpu_custom_call" | custom-call | tf_op jit(solution)/shard_map/exchange_py0/pallas_call | solution.py:110
  66.2 1.6 copy-done.2
  67.7 1.2 copy-done.11
  69.0 1.2 copy-done.12
  70.2 2.6 %y_forward.1 = f32[256,256]{1,0:T(8,128)S(1)} custom-call(f32[2048,256]{1,0:T(8,128)S(1)} %bitcast.12, bf16[256,2048]{1,0:T(8,128)(2,1)S(1)} %copy-done.12, bf16[256,2048]{1,0:T(8,128)(2,1)S(1)} %copy-done.11), custom_call_target="tpu_custom_call" | custom-call | tf_op jit(solution)/shard_map/y_forward/pallas_call | solution.py:247
  72.8 0.7 copy-done.13
  73.5 15.8 %exchange_pz1.1 = f32[32,8,256]{2,1,0:T(8,128)} custom-call(f32[32,8,256]{2,1,0:T(8,128)} %bitcast.14), custom_call_target="tpu_custom_call" | custom-call | tf_op jit(solution)/shard_map/exchange_pz1/pallas_call | solution.py:110
  89.4 1.4 copy-done.8
  90.8 0.9 copy-done.15
  91.7 1.1 copy-done.17
  92.9 6.3 %middle.1 = f32[256,256]{1,0:T(8,128)S(1)} custom-call(f32[256,256]{1,0:T(8,128)S(1)} %bitcast.16, bf16[2,192,1024]{2,1,0:T(8,128)(2,1)S(1)} %bitcast.18, bf16[8,384,256]{2,1,0:T(8,128)(2,1)S(1)} %copy-done.8, bf16[8,384,256]{2,1,0:T(8,128)(2,1)S(1)} %copy-done.7, bf16[8,256,384]{2,1,0:T(8,128)(2,1)S(1)} %copy-done.6, bf16[8,256,384]{2,1,0:T(8,128)(2,1)} %constant.28.clone.il_ref), custom_call_target="tpu_custom_call" | custom-call | tf_op jit(solution)/shard_map/middle/pallas_call | solution.py:265
  99.9 14.7 %exchange_pz2.1 = f32[32,8,256]{2,1,0:T(8,128)} custom-call(f32[32,8,256]{2,1,0:T(8,128)} %bitcast.17), custom_call_target="tpu_custom_call" | custom-call | tf_op jit(solution)/shard_map/exchange_pz2/pallas_call | solution.py:110
  114.6 1.2 copy-done.9
  115.8 1.2 copy-done.10
  117.0 0.9 copy-done.14
  118.0 2.2 %y_inverse.1 = f32[2048,256]{1,0:T(8,128)S(1)} custom-call(f32[256,256]{1,0:T(8,128)S(1)} %bitcast.15, bf16[2048,256]{1,0:T(8,128)(2,1)S(1)} %copy-done.10, bf16[2048,256]{1,0:T(8,128)(2,1)S(1)} %copy-done.9), custom_call_target="tpu_custom_call" | custom-call | tf_op jit(solution)/shard_map/y_inverse/pallas_call | solution.py:275
  120.2 1.3 copy-done.3
  121.5 55.9 %exchange_py3.1.r_ref = f32[16,16,8,256]{3,2,1,0:T(8,128)} custom-call(f32[16,16,8,256]{3,2,1,0:T(8,128)} %bitcast.13), custom_call_target="tpu_custom_call" | custom-call | tf_op jit(solution)/shard_map/exchange_py3/pallas_call | solution.py:110
  177.5 1.6 copy-done.4
  179.1 6.3 %x_inverse.1 = bf16[32,128,256]{2,1,0:T(8,128)(2,1)} custom-call(f32[16,16,8,256]{3,2,1,0:T(8,128)S(1)} %copy-done.4, bf16[32,128,256]{2,1,0:T(8,128)(2,1)S(1)} %bitcast.11, bf16[32,32]{1,0:T(8,128)(2,1)S(1)} %copy-done.21, f32[1,32]{1,0:T(1,128)S(1)} %bitcast.19, bf16[128,256]{1,0:T(8,128)(2,1)S(1)} %copy-done.20, bf16[128,256]{1,0:T(8,128)(2,1)S(1)} %copy-done.19), custom_call_target="tpu_custom_call" | custom-call | tf_op jit(solution)/shard_map/x_inverse/pallas_call | solution.py:292
  (31 shorter events, 0.8 us)
Async XLA Ops:
  0.0 1.6 copy-start
  1.6 0.9 copy-start.18
  5.0 1.3 copy-start.5
  66.2 1.6 copy-start.2
  67.7 1.2 copy-start.11
  69.0 1.2 copy-start.12
  70.2 19.2 %copy-start.6 = (bf16[8,256,384]{2,1,0:T(8,128)(2,1)S(1)}, bf16[8,256,384]{2,1,0:T(8,128)(2,1)}, u32[]{:S(2)}) copy-start(bf16[8,256,384]{2,1,0:T(8,128)(2,1)} %constant.27.clone.ih_ref) | copy-start | bytes 4718596
  70.2 19.2 %copy-start.7 = (bf16[8,384,256]{2,1,0:T(8,128)(2,1)S(1)}, bf16[8,384,256]{2,1,0:T(8,128)(2,1)}, u32[]{:S(2)}) copy-start(bf16[8,384,256]{2,1,0:T(8,128)(2,1)} %constant.26.clone.fl_ref) | copy-start | bytes 4718596
  72.8 0.7 copy-start.13
  89.4 1.4 copy-start.8
  90.8 0.9 copy-start.15
  91.7 1.1 copy-start.17
  99.2 0.7 copy-start.16
  114.6 1.2 copy-start.9
  115.8 1.2 copy-start.10
  117.0 0.9 copy-start.14
  120.2 1.3 copy-start.3
  121.5 55.9 %copy-start.1 = (bf16[32,16,8,256]{3,2,1,0:T(8,128)(2,1)S(1)}, bf16[32,16,8,256]{3,2,1,0:T(8,128)(2,1)}, u32[]{:S(2)}) copy-start(bf16[32,16,8,256]{3,2,1,0:T(8,128)(2,1)} %param.15) | copy-start | bytes 6291460
  121.5 55.9 %copy-start.19 = (bf16[128,256]{1,0:T(8,128)(2,1)S(1)}, bf16[128,256]{1,0:T(8,128)(2,1)}, u32[]{:S(2)}) copy-start(bf16[128,256]{1,0:T(8,128)(2,1)} %constant.32.clone.tl_ref) | copy-start | bytes 196612
  121.5 55.9 %copy-start.20 = (bf16[128,256]{1,0:T(8,128)(2,1)S(1)}, bf16[128,256]{1,0:T(8,128)(2,1)}, u32[]{:S(2)}) copy-start(bf16[128,256]{1,0:T(8,128)(2,1)} %constant.31.clone.th_ref) | copy-start | bytes 196612
  121.5 55.9 %copy-start.21 = (bf16[32,32]{1,0:T(8,128)(2,1)S(1)}, bf16[32,32]{1,0:T(8,128)(2,1)}, u32[]{:S(2)}) copy-start(bf16[32,32]{1,0:T(8,128)(2,1)} %w_ref.1) | copy-start | bytes 6148
  121.5 55.9 %copy-start.22 = (f32[32]{0:T(128)S(1)}, f32[32]{0:T(128)}, u32[]{:S(2)}) copy-start(f32[32]{0:T(128)} %param.18) | copy-start | bytes 388
  177.5 1.6 copy-start.4

commit v2 on v1

v2 whole, which is shorter than its diff:
```python
import functools
import math

import jax
import jax.numpy as jnp
import ml_dtypes
import numpy as np
from jax import lax
from jax.experimental import pallas as pl
from jax.experimental.pallas import tpu as pltpu
from jax.sharding import PartitionSpec as P

MESH = pl.DeviceIdType.MESH
BF = jnp.bfloat16
F32 = jnp.float32
MIB = 1 << 20
GROUP = 4


def centred(count):
    index = np.arange(count)
    return np.where(index < count // 2, index, index - count)


def split(table, axis=0):
    high = table.astype(ml_dtypes.bfloat16)
    low = (table - high.astype(np.float64)).astype(ml_dtypes.bfloat16)
    return np.stack([high, low], axis)


def pair(frequencies, positions, period, sign):
    angle = 2.0 * np.pi * ((positions[:, None] * frequencies[None, :]) % period) / period
    c, s = np.cos(angle), np.sin(angle)
    return np.stack([np.stack([c, sign * s]), np.stack([-sign * s, c])])


def make_tables(nx, ny, nz, mx, my, mz, py, pz):
    k = mx // py
    zl = nz // pz
    yl = ny // py
    norm = 1.0 / math.sqrt(nx * ny * nz)
    angle = 2.0 * np.pi * ((np.arange(mx)[:, None] * np.arange(nx)[None, :]) % nx) / nx
    eye = np.eye(k)
    xf = np.stack([np.cos(angle) * norm, -np.sin(angle) * norm], 1).reshape(2 * mx, nx)
    weight = np.where(np.arange(mx) == 0, 1.0, 2.0)[:, None] * norm
    xi = np.stack([np.cos(angle) * weight, -np.sin(angle) * weight], 1).reshape(2 * mx, nx)
    order = np.arange(my).reshape(pz // GROUP, GROUP).T.reshape(-1)
    yf = pair(centred(my), np.arange(ny), ny, -1.0)[..., order].reshape(2, 2, py, yl, my)
    yf = np.einsum("pqdyj,kl->djkqylp", yf, eye).reshape(py, my * k * 2, yl * k * 2)
    yi = pair(centred(my), np.arange(ny), ny, 1.0)[..., order].reshape(2, 2, py, yl, my)
    yi = np.einsum("qrdyj,kl->dykrjlq", yi, eye).reshape(py, yl * k * 2, my * k * 2)
    zf = pair(centred(mz), np.arange(nz), nz, -1.0).reshape(2, 2, pz, zl, mz)
    zf = np.einsum("pqszm,kl->zqkmslp", zf, eye).reshape(zl, 2 * k * mz, pz * k * 2)
    zi = pair(centred(mz), np.arange(nz), nz, 1.0).reshape(2, 2, pz, zl, mz)
    zi = np.einsum("qrszm,kl->zskrqlm", zi, eye).reshape(zl, pz * k * 2, 2 * k * mz)
    return xf, xi, yf, yi, zf, zi


def halves(value):
    high = value.astype(BF)
    return high, (value - high.astype(F32)).astype(BF)


def dot(a, b, dims=((1,), (0,))):
    return lax.dot_general(a, b, (dims, ((), ())), preferred_element_type=F32)


def dot3(ah, al, bh, bl):
    return dot(ah, bh) + dot(al, bh) + dot(ah, bl)


def x_forward(zl, field, table, out, first, last):
    def step(i, carry):
        block = field[:, pl.ds(pl.multiple_of(i * 2 * zl, 2 * zl), 2 * zl), :].astype(F32)
        channels, _, length = block.shape
        for y in range(2):
            plane = block[:, y * zl : (y + 1) * zl, :].reshape(channels * zl, length).astype(BF)
            both = dot(table[...], plane, ((1,), (1,)))
            half = both.shape[0] // 2
            rows = out.shape[1] // (field.shape[1] // zl)
            start = pl.multiple_of((i * 2 + y) * rows, rows)
            out[:, pl.ds(start, rows), :] = (both[:half] + both[half:]).reshape(
                out.shape[0], rows, out.shape[2]
            )
        return carry

    lax.fori_loop(first, last, step, 0)


def middle(zl, x, w, forward, inverse):
    xh, xl = halves(x)
    lanes = x.shape[1]
    channels = lanes // zl
    inner = lax.broadcasted_iota(jnp.int32, (1, lanes), 1) % zl
    modes = jnp.zeros((forward.shape[2], lanes), F32)
    for z in range(zl):
        modes += jnp.where(inner == z, dot3(forward[z, 0], forward[z, 1], xh, xl), 0.0)
    pairs = w.shape[2]
    lane = lax.broadcasted_iota(jnp.int32, (lanes, pairs), 0) // zl
    both = lax.broadcasted_iota(jnp.int32, (lanes, pairs), 1)
    spread = jnp.where(lane == both // channels, 1.0, 0.0).astype(BF)
    mh, ml = halves(modes)
    wide = dot(mh, spread) + dot(ml, spread)
    half = wide.shape[0] // 2
    re, im = wide[:half], wide[half:]
    wr, wi = w[0].astype(F32), w[1].astype(F32)
    mixed = jnp.concatenate([wr * re - wi * im, wr * im + wi * re], axis=0)
    both = lax.broadcasted_iota(jnp.int32, (pairs, lanes), 0)
    lane = lax.broadcasted_iota(jnp.int32, (pairs, lanes), 1) // zl
    gather = jnp.where(both % channels == lane, 1.0, 0.0).astype(BF)
    ph, plo = halves(mixed)
    summed = dot(ph, gather) + dot(plo, gather)
    sh, sl = halves(summed)
    total = jnp.zeros(x.shape, F32)
    for z in range(zl):
        total += jnp.where(inner == z, dot3(inverse[z, 0], inverse[z, 1], sh, sl), 0.0)
    return total


def spectrum_kernel(n_y, n_z, zl, *refs):
    (
        f_hbm, xt_hbm, yt_hbm, yi_hbm, zf_hbm, zi_hbm, w_hbm, r_hbm,
        f, xt, yt, yi, zf, zi, w, a, theirs, summing, arrived, total, seen, mixed, back, ring, planes,
        load_sem, swap_s, swap_r, sum_s, sum_r, out_s, out_r, in_s, in_r, ring_s, ring_r,
        turn_s, turn_r, keep_s,
    ) = refs
    here, column = lax.axis_index("py"), lax.axis_index("pz")
    n_ring = n_y // 2
    side, z = here // n_ring, here % n_ring
    other = 1 - side
    half_py = lambda s, at: s * n_ring + at % n_ring
    partner = {"py": half_py(other, z)}
    neighbours = ({"py": half_py(side, z + 1)}, {"py": half_py(side, z + n_ring - 1)})

    loads = []

    def load(source, target):
        copy = pltpu.make_async_copy(source, target, load_sem.at[len(loads)])
        copy.start()
        loads.append(copy)
        return copy

    pieces = 4
    rows = f.shape[1] // pieces
    table_x = load(xt_hbm, xt)
    fields = [
        load(f_hbm.at[:, pl.ds(i * rows, rows), :], f.at[:, pl.ds(i * rows, rows), :])
        for i in range(pieces)
    ]
    depth = yt_hbm.shape[3]
    table_y = [
        load(yt_hbm.at[half_py(s, z)], yt.at[:, :, pl.ds(i * depth, depth)])
        for i, s in enumerate((side, other))
    ]
    table_z = [load(zf_hbm, zf), load(w_hbm, w), load(zi_hbm, zi)]
    table_i = [load(yi_hbm.at[half_py(s, z)], yi.at[i]) for i, s in enumerate((side, other))]

    barrier = pltpu.get_barrier_semaphore()
    for peer in (partner,) + neighbours:
        pl.semaphore_signal(barrier, inc=1, device_id=peer, device_id_type=MESH)

    def greet(step, carry):
        pl.semaphore_signal(
            barrier, inc=1, device_id={"pz": (column + step) % n_z}, device_id_type=MESH
        )
        return carry

    lax.fori_loop(1, n_z, greet, 0)

    table_x.wait()
    turns = f.shape[1] // (2 * zl) // pieces
    for i in range(pieces):
        fields[i].wait()
        x_forward(zl, f, xt, a, i * turns, (i + 1) * turns)
    pl.semaphore_wait(barrier, n_z + 2)

    reach = n_ring // 2
    offsets = [reach] + [o * s for o in range(reach - 1, 0, -1) for s in (1, -1)] + [0]

    def swap(i):
        at = (z + offsets[i] + n_ring) % n_ring
        return pltpu.make_async_remote_copy(
            src_ref=a.at[half_py(other, at)],
            dst_ref=theirs.at[at],
            send_sem=swap_s.at[i],
            recv_sem=swap_r.at[i],
            device_id=partner,
            device_id_type=MESH,
        )

    for i in range(n_ring):
        swap(i).start()
    for copy in table_y:
        copy.wait()

    def partial(i):
        at = (z + offsets[i] + n_ring) % n_ring
        swap(i).wait_recv()
        block = jnp.concatenate([a[half_py(side, at)], theirs[at]], axis=0)
        high, low = halves(block)
        return dot3(yt[0], yt[1], high, low)

    part = total.shape[0] * total.shape[1] // GROUP
    span = lambda g: pl.ds(g * part, part)
    carries = lambda way, step, g: step > 0 or (g < GROUP // 2) == (way == 0)

    def hop(way, step, g):
        index = (way * reach + step) * GROUP + g
        return pltpu.make_async_remote_copy(
            src_ref=summing.at[way, step, span(g)],
            dst_ref=arrived.at[way, step, span(g)],
            send_sem=sum_s.at[index],
            recv_sem=sum_r.at[index],
            device_id=neighbours[way],
            device_id_type=MESH,
        )

    block = partial(0)
    for g in range(GROUP):
        way = 0 if g < GROUP // 2 else 1
        summing[way, 0, g * part : (g + 1) * part] = block[g * part : (g + 1) * part]
        hop(way, 0, g).start()
    for step in range(1, reach):
        for way in range(2):
            summing[way, step] = partial(2 * step - 1 + way)
        for g in range(GROUP):
            for way in range(2):
                if carries(way, step - 1, g):
                    hop(way, step - 1, g).wait_recv()
                    summing[way, step, span(g)] += arrived[way, step - 1, span(g)]
                hop(way, step, g).start()

    per = n_z // GROUP
    y_chip, place = column // GROUP, column % GROUP
    slot = place * per + y_chip
    last = partial(n_ring - 1)

    def to_owner(source, owner):
        return pltpu.make_async_remote_copy(
            src_ref=total.at[source],
            dst_ref=seen.at[column],
            send_sem=out_s.at[owner],
            recv_sem=out_r.at[column],
            device_id={"pz": owner},
            device_id_type=MESH,
        )

    def from_owner(owner):
        return pltpu.make_async_remote_copy(
            src_ref=total.at[0],
            dst_ref=seen.at[owner],
            send_sem=out_s.at[owner],
            recv_sem=out_r.at[owner],
            device_id={"pz": owner},
            device_id_type=MESH,
        )

    for g in range(GROUP):
        for way in range(2):
            hop(way, reach - 1, g).wait_recv()
        value = last[g * part : (g + 1) * part] + arrived[0, reach - 1, span(g)]
        value = value + arrived[1, reach - 1, span(g)]
        total[g * per : (g + 1) * per] = value.reshape(per, total.shape[1], total.shape[2])

        def send(i, carry):
            chip = (y_chip + i) % per
            owner = chip * GROUP + g

            @pl.when(owner != column)
            def _():
                to_owner(g * per + chip, owner).start()

            return carry

        lax.fori_loop(0, per, send, 0)
    seen[column] = total[slot]

    def collect(step, carry):
        from_owner((column + step) % n_z).wait()
        return carry

    for copy in table_z:
        copy.wait()
    lax.fori_loop(1, n_z, collect, 0)

    value = middle(zl, seen[...].reshape(-1, seen.shape[2]), w, zf, zi)
    mixed[...] = value.reshape(mixed.shape)

    def to_cells(step):
        peer = (column + step) % n_z
        return pltpu.make_async_remote_copy(
            src_ref=mixed.at[peer],
            dst_ref=back.at[slot],
            send_sem=in_s.at[step],
            recv_sem=in_r.at[step],
            device_id={"pz": peer},
            device_id_type=MESH,
        )

    def start_back(step, carry):
        to_cells(step).start()
        return carry

    def end_back(step, carry):
        to_cells(step).wait()
        return carry

    lax.fori_loop(1, n_z, start_back, 0)
    back[slot] = mixed[column]
    for copy in table_i:
        copy.wait()
    lax.fori_loop(1, n_z, end_back, 0)

    wide = lambda g: pl.ds(g * per, per)
    passes = lambda way, step, g: step < reach - 1 or (g < GROUP // 2) == (way == 0)

    def relay(way, step, g):
        index = (way * reach + step) * GROUP + g
        source = back.at[wide(g)] if step == 0 else ring.at[way, step - 1, wide(g)]
        target = ring.at[0 if step == reach - 1 else way, step, wide(g)]
        return pltpu.make_async_remote_copy(
            src_ref=source,
            dst_ref=target,
            send_sem=ring_s.at[index],
            recv_sem=ring_r.at[index],
            device_id=neighbours[way],
            device_id_type=MESH,
        )

    def turn(i, owner):
        return pltpu.make_async_remote_copy(
            src_ref=planes.at[1, i],
            dst_ref=r_hbm.at[owner],
            send_sem=turn_s.at[i],
            recv_sem=turn_r.at[i],
            device_id=partner,
            device_id_type=MESH,
        )

    def keep(i, owner):
        return pltpu.make_async_copy(planes.at[0, i], r_hbm.at[owner], keep_s.at[i])

    def spread(i, offset, block):
        owner = half_py(side, z + offset + n_ring)
        high, low = halves(block.reshape(-1, block.shape[2]))
        planes[1, i] = dot3(yi[1, 0], yi[1, 1], high, low)
        turn(i, owner).start()
        planes[0, i] = dot3(yi[0, 0], yi[0, 1], high, low)
        keep(i, owner).start()

    for g in range(GROUP):
        for way in range(2):
            relay(way, 0, g).start()
    spread(0, 0, back[...])
    for step in range(1, reach):
        for g in range(GROUP):
            for way in range(2):
                relay(way, step - 1, g).wait_recv()
                if passes(way, step, g):
                    relay(way, step, g).start()
        for way in range(2):
            spread(2 * step - 1 + way, step if way else -step, ring[way, step - 1])
    for g in range(GROUP):
        for way in range(2):
            if passes(way, reach - 1, g):
                relay(way, reach - 1, g).wait_recv()
    spread(n_ring - 1, reach, ring[0, reach - 1])

    for i in range(n_ring):
        swap(i).wait_send()
    for step in range(reach):
        for g in range(GROUP):
            for way in range(2):
                if carries(way, step, g):
                    hop(way, step, g).wait_send()
                if passes(way, step, g):
                    relay(way, step, g).wait_send()
    for i in range(n_ring):
        keep(i, here).wait()
        turn(i, here).wait()


def x_inverse_kernel(zl, r_ref, f_ref, w_ref, b_ref, th_ref, tl_ref, o_ref, mix_ref, bias_ref):
    channels, rows, length = f_ref.shape
    lanes = channels * zl

    @pl.when(pl.program_id(0) == 0)
    def _():
        row = lax.broadcasted_iota(jnp.int32, (lanes, channels), 0) // zl
        column = lax.broadcasted_iota(jnp.int32, (lanes, channels), 1)
        pick = row == column
        ones = jnp.where(pick, 1.0, 0.0).astype(BF)
        left = dot(ones, w_ref[...], ((1,), (1,))).astype(BF)
        full = dot(left, ones, ((1,), (1,)))
        a = lax.broadcasted_iota(jnp.int32, (lanes, lanes), 0) % zl
        b = lax.broadcasted_iota(jnp.int32, (lanes, lanes), 1) % zl
        mix_ref[...] = jnp.where(a == b, full, 0.0).astype(BF)
        column = jnp.sum(jnp.where(pick, b_ref[...], 0.0), axis=1, keepdims=True)
        bias_ref[...] = jnp.broadcast_to(column, bias_ref.shape)

    block = f_ref[...].astype(F32)
    th, tl, mix, bias = th_ref[...], tl_ref[...], mix_ref[...], bias_ref[...]
    for y in range(rows // zl):
        spectrum = r_ref[:, y].reshape(-1, lanes)
        sh, sl = halves(spectrum)
        field = block[:, y * zl : (y + 1) * zl, :].reshape(lanes, length).astype(BF)
        first = ((0,), (0,))
        value = dot(sh, th, first) + dot(sl, th, first) + dot(sh, tl, first)
        value = value + dot(mix, field) + bias
        out = jax.nn.gelu(value).reshape(channels, zl, length)
        o_ref[:, y * zl : (y + 1) * zl, :] = out.astype(o_ref.dtype)


def params(mib):
    return pltpu.CompilerParams(vmem_limit_bytes=mib * MIB)


def whole(shape):
    return pl.BlockSpec(shape, lambda i: (0,) * len(shape))


def per_device(tables, n_y, n_z, features, spectral_weight, bypass_weight, bias_vector):
    xf, xi, yf, yi, zf, zi = tables
    c, yl, zl, nx = features.shape
    _, kl, _, mz, pairs = spectral_weight.shape
    lanes = c * zl
    part = 2 * kl
    rows = yl * part
    flat = features.reshape(c, yl * zl, nx)
    x_rows = split(xf).reshape(-1, nx)
    y_rows, y_back = split(yf, 1), split(yi, 1)
    z_rows, z_back = split(zf, 1), split(zi, 1)
    weight = spectral_weight.reshape(2, kl * mz, pairs)
    my_rows = y_rows.shape[2]
    modes = my_rows // part
    n_ring = n_y // 2
    reach = n_ring // 2
    operands = [flat] + [jnp.asarray(t) for t in (x_rows, y_rows, y_back, z_rows, z_back)] + [weight]
    sems = [16, n_ring, n_ring] + [2 * reach * GROUP] * 2 + [n_z] * 4 + [2 * reach * GROUP] * 2
    sems += [n_ring] * 3
    planes = pl.pallas_call(
        functools.partial(spectrum_kernel, n_y, n_z, zl),
        out_shape=jax.ShapeDtypeStruct((n_y, rows, lanes), F32),
        in_specs=[pl.BlockSpec(memory_space=pl.ANY)] * len(operands),
        out_specs=pl.BlockSpec(memory_space=pl.ANY),
        scratch_shapes=[
            pltpu.VMEM(flat.shape, BF),
            pltpu.VMEM(x_rows.shape, BF),
            pltpu.VMEM((2, my_rows, 2 * rows), BF),
            pltpu.VMEM((2,) + y_back.shape[1:], BF),
            pltpu.VMEM(z_rows.shape, BF),
            pltpu.VMEM(z_back.shape, BF),
            pltpu.VMEM(weight.shape, BF),
            pltpu.VMEM((n_y, rows, lanes), F32),
            pltpu.VMEM((n_ring, rows, lanes), F32),
            pltpu.VMEM((2, reach, my_rows, lanes), F32),
            pltpu.VMEM((2, reach, my_rows, lanes), F32),
            pltpu.VMEM((modes, part, lanes), F32),
            pltpu.VMEM((n_z, part, lanes), F32),
            pltpu.VMEM((n_z, part, lanes), F32),
            pltpu.VMEM((modes, part, lanes), F32),
            pltpu.VMEM((2, reach, modes, part, lanes), F32),
            pltpu.VMEM((2, n_ring, rows, lanes), F32),
        ]
        + [pltpu.SemaphoreType.DMA((n,)) for n in sems],
        compiler_params=pltpu.CompilerParams(
            collective_id=0, has_side_effects=True, vmem_limit_bytes=60 * MIB
        ),
        name="spectrum",
    )(*operands)

    step = 2
    steps = yl // step
    field_spec = pl.BlockSpec((c, step * zl, nx), lambda i: (0, i, 0))
    th, tl = map(jnp.asarray, split(xi))
    out = pl.pallas_call(
        functools.partial(x_inverse_kernel, zl),
        grid=(steps,),
        in_specs=[
            pl.BlockSpec((n_y, step, part, lanes), lambda i: (0, i, 0, 0)),
            field_spec,
            whole(bypass_weight.shape),
            whole((1, c)),
            whole(th.shape),
            whole(tl.shape),
        ],
        out_specs=field_spec,
        out_shape=jax.ShapeDtypeStruct(flat.shape, BF),
        scratch_shapes=[pltpu.VMEM((lanes, lanes), BF), pltpu.VMEM((lanes, nx), F32)],
        compiler_params=params(60),
        name="x_inverse",
    )(planes.reshape(n_y, yl, part, lanes), flat, bypass_weight, bias_vector.reshape(1, c), th, tl)
    return out.reshape(features.shape)


def solution(mesh):
    n_y, n_z = mesh.shape["py"], mesh.shape["pz"]

    def run(features, spectral_weight, bypass_weight, bias_vector):
        _, ny, nz, nx = features.shape
        _, mx, my, mz, _ = spectral_weight.shape
        tables = make_tables(nx, ny, nz, mx, my, mz, n_y, n_z)
        return jax.shard_map(
            functools.partial(per_device, tables, n_y, n_z),
            mesh=mesh,
            in_specs=(P(None, "py", "pz", None), P(None, "py", "pz", None, None), P(), P()),
            out_specs=P(None, "py", "pz", None),
            check_vma=False,
        )(features, spectral_weight, bypass_weight, bias_vector)

    return run
```

time: 187 us -> 107 us (0.57)
  Pallas kernels: 166 us -> 107 us
  local copies, waits for them, and re-layouts: 19 us -> 0 us
    pallas_call x8 -> x1, Pallas kernels: 160 us -> 98 us  [per_device(): pl.pallas_call(functools.partial(spectrum_kernel, n_y, n_z, zl), out_shap...]
    unnamed x46 -> x0, local copies, waits for them, and re-layouts: 19 us -> none
    pallas_call x1, Pallas kernels: 6.27 us -> 8.63 us  [per_device(): pl.pallas_call(functools.partial(x_inverse_kernel, zl), grid=(steps,), in...]
where the time goes in v2:
time: 107 us
  Pallas kernels  107 us (100%)
    pallas_call x1, Pallas kernels, per_device(): pl.pallas_call(functools.partial(spectrum_kernel, n_y, n_z, zl), out_shap...  98 us
    pallas_call x1, Pallas kernels, per_device(): pl.pallas_call(functools.partial(x_inverse_kernel, zl), grid=(steps,), in...  8.63 us

profile of v2, /device:TPU:6, one launch (start us, length us, event | category | flops | bytes accessed | tf_op | source)
XLA Modules:
  0.0 106.7 jit_solution(14504402083058986737)
XLA Ops:
  0.0 98.0 %spectrum.1 = f32[16,128,256]{2,1,0:T(8,128)} custom-call(bf16[32,128,256]{2,1,0:T(8,128)(2,1)} %bitcast.5, bf16[256,256]{1,0:T(8,128)(2,1)} %constant.14.clone.refs_1_, bf16[16,2,256,128]{3,2,1,0:T(8,128)(2,1)} %constant.15.clone.refs_2_, bf16[16,2,128,256]{3,2,1,0:T(8,128)(2,1)} %constant.16.clone.refs_3_, ...), custom_call_target="tpu_custom_call" | custom-call | tf_op jit(solution)/shard_map/spectrum/pallas_call | solution.py:441
  98.1 8.6 %x_inverse.1 = bf16[32,128,256]{2,1,0:T(8,128)(2,1)} custom-call(f32[16,16,8,256]{3,2,1,0:T(8,128)} %bitcast.7, bf16[32,128,256]{2,1,0:T(8,128)(2,1)} %bitcast.6, bf16[32,32]{1,0:T(8,128)(2,1)} %w_ref.1, f32[1,32]{1,0:T(1,128)} %bitcast.9, bf16[128,256]{1,0:T(8,128)(2,1)} %constant.19.clone.th_ref, bf16[128,256]{1,0:T(8,128)(2,1)} %constant.20.clone.tl_ref), custom_call_target="tpu_custom_call" | custom-call | tf_op jit(solution)/shard_map/x_inverse/pallas_call | solution.py:476

commit v3 on v2

--- a/solution.py
+++ b/solution.py
@@ -26,6 +26,11 @@
     high = table.astype(ml_dtypes.bfloat16)
     low = (table - high.astype(np.float64)).astype(ml_dtypes.bfloat16)
     return np.stack([high, low], axis)
+
+
+def thrice(table):
+    high, low = split(table)
+    return np.concatenate([high, high, low], -1)
 
 
 def pair(frequencies, positions, period, sign):
@@ -50,15 +55,20 @@
     yi = pair(centred(my), np.arange(ny), ny, 1.0)[..., order].reshape(2, 2, py, yl, my)
     yi = np.einsum("qrdyj,kl->dykrjlq", yi, eye).reshape(py, yl * k * 2, my * k * 2)
     zf = pair(centred(mz), np.arange(nz), nz, -1.0).reshape(2, 2, pz, zl, mz)
-    zf = np.einsum("pqszm,kl->zqkmslp", zf, eye).reshape(zl, 2 * k * mz, pz * k * 2)
-    zi = pair(centred(mz), np.arange(nz), nz, 1.0).reshape(2, 2, pz, zl, mz)
-    zi = np.einsum("qrszm,kl->zskrqlm", zi, eye).reshape(zl, pz * k * 2, 2 * k * mz)
+    zf = np.einsum("pqszm->zqmps", zf).reshape(zl, 2 * mz, 2 * pz)
+    zi = pair(centred(mz), np.arange(nz), nz, 1.0).reshape(2, 2, pz // GROUP, GROUP, zl, mz)
+    zi = np.einsum("qrjgzm->gzrjqm", zi).reshape(GROUP, zl * 2 * pz // GROUP, 2 * mz)
     return xf, xi, yf, yi, zf, zi
 
 
 def halves(value):
     high = value.astype(BF)
     return high, (value - high.astype(F32)).astype(BF)
+
+
+def triple(value):
+    high, low = halves(value)
+    return jnp.concatenate([high, low, high], 0)
 
 
 def dot(a, b, dims=((1,), (0,))):
@@ -87,14 +97,25 @@
     lax.fori_loop(first, last, step, 0)
 
 
-def middle(zl, x, w, forward, inverse):
-    xh, xl = halves(x)
-    lanes = x.shape[1]
+def middle(zl, x, w, forward):
+    cells, part, lanes = x.shape
+    kl = part // 2
     channels = lanes // zl
-    inner = lax.broadcasted_iota(jnp.int32, (1, lanes), 1) % zl
-    modes = jnp.zeros((forward.shape[2], lanes), F32)
+    column = lambda k: jnp.concatenate([x[:, 2 * k, :], x[:, 2 * k + 1, :]], axis=0)
+    block = triple(jnp.concatenate([column(k) for k in range(kl)], axis=1))
+    inner = lax.broadcasted_iota(jnp.int32, (1, kl * lanes), 1) % zl
+    modes = jnp.zeros((forward.shape[1], kl * lanes), F32)
     for z in range(zl):
-        modes += jnp.where(inner == z, dot3(forward[z, 0], forward[z, 1], xh, xl), 0.0)
+        modes += jnp.where(inner == z, dot(forward[z], block), 0.0)
+    count = modes.shape[0] // 2
+    modes = jnp.concatenate(
+        [
+            modes[p * count : (p + 1) * count, k * lanes : (k + 1) * lanes]
+            for p in range(2)
+            for k in range(kl)
+        ],
+        axis=0,
+    )
     pairs = w.shape[2]
     lane = lax.broadcasted_iota(jnp.int32, (lanes, pairs), 0) // zl
     both = lax.broadcasted_iota(jnp.int32, (lanes, pairs), 1)
@@ -110,11 +131,9 @@
     gather = jnp.where(both % channels == lane, 1.0, 0.0).astype(BF)
     ph, plo = halves(mixed)
     summed = dot(ph, gather) + dot(plo, gather)
-    sh, sl = halves(summed)
-    total = jnp.zeros(x.shape, F32)
-    for z in range(zl):
-        total += jnp.where(inner == z, dot3(inverse[z, 0], inverse[z, 1], sh, sl), 0.0)
-    return total
+    row = lambda p, k: summed[(p * kl + k) * count : (p * kl + k + 1) * count]
+    columns = [jnp.concatenate([row(0, k), row(1, k)], axis=0) for k in range(kl)]
+    return triple(jnp.concatenate(columns, axis=1))
 
 
 def spectrum_kernel(n_y, n_z, zl, *refs):
@@ -283,30 +302,51 @@
         copy.wait()
     lax.fori_loop(1, n_z, collect, 0)
 
-    value = middle(zl, seen[...].reshape(-1, seen.shape[2]), w, zf, zi)
-    mixed[...] = value.reshape(mixed.shape)
-
-    def to_cells(step):
+    modes = middle(zl, seen, w, zf)
+    lanes = seen.shape[2]
+    kl = seen.shape[1] // 2
+    inner = lax.broadcasted_iota(jnp.int32, (1, modes.shape[1]), 1) % zl
+
+    def to_cells(source, peer, target, sender):
+        return pltpu.make_async_remote_copy(
+            src_ref=mixed.at[source],
+            dst_ref=back.at[target],
+            send_sem=in_s.at[peer],
+            recv_sem=in_r.at[sender],
+            device_id={"pz": peer},
+            device_id_type=MESH,
+        )
+
+    for g in range(GROUP):
+        value = dot(zi[g], modes)
+        size = 2 * per
+        cells = jnp.zeros((size, modes.shape[1]), F32)
+        for i in range(zl):
+            cells += jnp.where(inner == i, value[i * size : (i + 1) * size], 0.0)
+        for p in range(2):
+            for k in range(kl):
+                mixed[g * per : (g + 1) * per, 2 * k + p, :] = cells[
+                    p * per : (p + 1) * per, k * lanes : (k + 1) * lanes
+                ]
+
+        def send_back(i, carry):
+            chip = (y_chip + i) % per
+            peer = chip * GROUP + g
+
+            @pl.when(peer != column)
+            def _():
+                to_cells(g * per + chip, peer, slot, column).start()
+
+            return carry
+
+        lax.fori_loop(0, per, send_back, 0)
+
+    def end_back(step, carry):
         peer = (column + step) % n_z
-        return pltpu.make_async_remote_copy(
-            src_ref=mixed.at[peer],
-            dst_ref=back.at[slot],
-            send_sem=in_s.at[step],
-            recv_sem=in_r.at[step],
-            device_id={"pz": peer},
-            device_id_type=MESH,
-        )
-
-    def start_back(step, carry):
-        to_cells(step).start()
+        to_cells(0, peer, 0, peer).wait()
         return carry
 
-    def end_back(step, carry):
-        to_cells(step).wait()
-        return carry
-
-    lax.fori_loop(1, n_z, start_back, 0)
-    back[slot] = mixed[column]
+    back[slot] = mixed[slot]
     for copy in table_i:
         copy.wait()
     lax.fori_loop(1, n_z, end_back, 0)
@@ -405,7 +445,7 @@
         sh, sl = halves(spectrum)
         field = block[:, y * zl : (y + 1) * zl, :].reshape(lanes, length).astype(BF)
         first = ((0,), (0,))
-        value = dot(sh, th, first) + dot(sl, th, first) + dot(sh, tl, first)
+        value = dot(jnp.concatenate([sh, sl], 0), th, first) + dot(sh, tl, first)
         value = value + dot(mix, field) + bias
         out = jax.nn.gelu(value).reshape(channels, zl, length)
         o_ref[:, y * zl : (y + 1) * zl, :] = out.astype(o_ref.dtype)
@@ -429,7 +469,7 @@
     flat = features.reshape(c, yl * zl, nx)
     x_rows = split(xf).reshape(-1, nx)
     y_rows, y_back = split(yf, 1), split(yi, 1)
-    z_rows, z_back = split(zf, 1), split(zi, 1)
+    z_rows, z_back = thrice(zf), thrice(zi)
     weight = spectral_weight.reshape(2, kl * mz, pairs)
     my_rows = y_rows.shape[2]
     modes = my_rows // part
@@ -464,15 +504,16 @@
         ]
         + [pltpu.SemaphoreType.DMA((n,)) for n in sems],
         compiler_params=pltpu.CompilerParams(
-            collective_id=0, has_side_effects=True, vmem_limit_bytes=60 * MIB
+            collective_id=0, has_side_effects=True, vmem_limit_bytes=62 * MIB
         ),
         name="spectrum",
     )(*operands)
 
-    step = 2
+    step = 4
     steps = yl // step
     field_spec = pl.BlockSpec((c, step * zl, nx), lambda i: (0, i, 0))
-    th, tl = map(jnp.asarray, split(xi))
+    high, tl = split(xi)
+    th = np.concatenate([high, high], 0)
     out = pl.pallas_call(
         functools.partial(x_inverse_kernel, zl),
         grid=(steps,),
@@ -487,9 +528,9 @@
         out_specs=field_spec,
         out_shape=jax.ShapeDtypeStruct(flat.shape, BF),
         scratch_shapes=[pltpu.VMEM((lanes, lanes), BF), pltpu.VMEM((lanes, nx), F32)],
-        compiler_params=params(60),
+        compiler_params=params(62),
         name="x_inverse",
-    )(planes.reshape(n_y, yl, part, lanes), flat, bypass_weight, bias_vector.reshape(1, c), th, tl)
+    )(planes.reshape(n_y, yl, part, lanes), flat, bypass_weight, bias_vector.reshape(1, c), jnp.asarray(th), jnp.asarray(tl))
     return out.reshape(features.shape)
 
 

time: 107 us -> 103 us (0.963)
  Pallas kernels: 107 us -> 102 us
    pallas_call x1, Pallas kernels: 98 us -> 95.6 us  [per_device(): pl.pallas_call(functools.partial(spectrum_kernel, n_y, n_z, zl), out_shap...]
    pallas_call x1, Pallas kernels: 8.63 us -> 6.45 us  [per_device(): pl.pallas_call(functools.partial(x_inverse_kernel, zl), grid=(steps,), in...]
where the time goes in v3:
time: 103 us; the launch traced here: 102 us
  Pallas kernels  102 us (99%)
    pallas_call x1, Pallas kernels, per_device(): pl.pallas_call(functools.partial(spectrum_kernel, n_y, n_z, zl), out_shap...  95.6 us
    pallas_call x1, Pallas kernels, per_device(): pl.pallas_call(functools.partial(x_inverse_kernel, zl), grid=(steps,), in...  6.45 us

profile of v3, /device:TPU:6, one launch (start us, length us, event | category | flops | bytes accessed | tf_op | source)
XLA Modules:
  0.0 102.1 jit_solution(15748248515261745007)
XLA Ops:
  0.0 95.6 %spectrum.1 = f32[16,128,256]{2,1,0:T(8,128)} custom-call(bf16[32,128,256]{2,1,0:T(8,128)(2,1)} %bitcast.5, bf16[256,256]{1,0:T(8,128)(2,1)} %constant.14.clone.refs_1_, bf16[16,2,256,128]{3,2,1,0:T(8,128)(2,1)} %constant.15.clone.refs_2_, bf16[16,2,128,256]{3,2,1,0:T(8,128)(2,1)} %constant.16.clone.refs_3_, bf16[8,96,192]{2,1,0:T(8,128)(2,1)} %constant.17.clone.refs_4_, ...), custom_call_target="tpu_custom_call" | custom-call | tf_op jit(solution)/shard_map/spectrum/pallas_call | solution.py:481
  95.6 6.5 %x_inverse.1 = bf16[32,128,256]{2,1,0:T(8,128)(2,1)} custom-call(f32[16,16,8,256]{3,2,1,0:T(8,128)} %bitcast.7, bf16[32,128,256]{2,1,0:T(8,128)(2,1)} %bitcast.6, bf16[32,32]{1,0:T(8,128)(2,1)} %w_ref.1, f32[1,32]{1,0:T(1,128)} %bitcast.9, bf16[256,256]{1,0:T(8,128)(2,1)} %constant.19.clone.th_ref, bf16[128,256]{1,0:T(8,128)(2,1)} %constant.20.clone.tl_ref), custom_call_target="tpu_custom_call" | custom-call | tf_op jit(solution)/shard_map/x_inverse/pallas_call | solution.py:517

commit v4 on v3

v4 whole, which is shorter than its diff:
```python
import functools
import math

import jax
import jax.numpy as jnp
import ml_dtypes
import numpy as np
from jax import lax
from jax.experimental import pallas as pl
from jax.experimental.pallas import tpu as pltpu
from jax.sharding import PartitionSpec as P

MESH = pl.DeviceIdType.MESH
BF = jnp.bfloat16
F32 = jnp.float32
MIB = 1 << 20
HALVES = 2
GROUP = 4


def centred(count):
    index = np.arange(count)
    return np.where(index < count // 2, index, index - count)


def split(table, axis=0):
    high = table.astype(ml_dtypes.bfloat16)
    low = (table - high.astype(np.float64)).astype(ml_dtypes.bfloat16)
    return np.stack([high, low], axis)


def thrice(table):
    high, low = split(table)
    return np.concatenate([high, high, low], -1)


def pair(frequencies, positions, period, sign):
    angle = 2.0 * np.pi * ((positions[:, None] * frequencies[None, :]) % period) / period
    c, s = np.cos(angle), np.sin(angle)
    return np.stack([np.stack([c, sign * s]), np.stack([-sign * s, c])])


def make_tables(nx, ny, nz, mx, my, mz, py, pz):
    k = mx // py
    zl = nz // pz
    yl = ny // py
    norm = 1.0 / math.sqrt(nx * ny * nz)
    angle = 2.0 * np.pi * ((np.arange(mx)[:, None] * np.arange(nx)[None, :]) % nx) / nx
    eye = np.eye(k)
    xf = np.stack([np.cos(angle) * norm, -np.sin(angle) * norm], 1).reshape(2 * mx, nx)
    weight = np.where(np.arange(mx) == 0, 1.0, 2.0)[:, None] * norm
    xi = np.stack([np.cos(angle) * weight, -np.sin(angle) * weight], 1).reshape(2 * mx, nx)
    order = np.arange(my).reshape(pz // GROUP, GROUP).T.reshape(-1)
    yf = pair(centred(my), np.arange(ny), ny, -1.0)[..., order].reshape(2, 2, py, yl, my)
    yf = np.einsum("pqdyj,kl->djkqylp", yf, eye).reshape(py, my * k * 2, yl * k * 2)
    yi = pair(centred(my), np.arange(ny), ny, 1.0)[..., order].reshape(2, 2, py, yl, my)
    yi = np.einsum("qrdyj,kl->dykrjlq", yi, eye).reshape(py, yl * k * 2, my * k * 2)
    zf = pair(centred(mz), np.arange(nz), nz, -1.0).reshape(2, 2, pz, zl, mz)
    zf = np.einsum("pqszm->zqmps", zf).reshape(zl, 2 * mz, 2 * pz)
    zi = pair(centred(mz), np.arange(nz), nz, 1.0).reshape(2, 2, pz // GROUP, GROUP, zl, mz)
    zi = np.einsum("qrjgzm->gzrjqm", zi).reshape(GROUP, zl * 2 * pz // GROUP, 2 * mz)
    return xf, xi, yf, yi, zf, zi


def halves(value):
    high = value.astype(BF)
    return high, (value - high.astype(F32)).astype(BF)


def triple(value):
    high, low = halves(value)
    return jnp.concatenate([high, low, high], 0)


def dot(a, b, dims=((1,), (0,))):
    return lax.dot_general(a, b, (dims, ((), ())), preferred_element_type=F32)


def dot3(ah, al, bh, bl):
    return dot(ah, bh) + dot(al, bh) + dot(ah, bl)


def x_forward(zl, field, table, out, h, first, last):
    channels = field.shape[0] // HALVES
    rows = out.shape[2] // (field.shape[1] // zl)

    def step(i, carry):
        start = pl.multiple_of(i * 2 * zl, 2 * zl)
        block = field[h * channels : (h + 1) * channels, pl.ds(start, 2 * zl), :].astype(F32)
        for y in range(2):
            plane = block[:, y * zl : (y + 1) * zl, :].reshape(channels * zl, -1).astype(BF)
            both = dot(table[...], plane, ((1,), (1,)))
            half = both.shape[0] // 2
            at = pl.multiple_of((i * 2 + y) * rows, rows)
            out[h, :, pl.ds(at, rows), :] = (both[:half] + both[half:]).reshape(
                out.shape[1], rows, out.shape[3]
            )
        return carry

    lax.fori_loop(first, last, step, 0)


def mix_modes(zl, x, w, forward, h):
    cells, part, lanes = x.shape
    kl = part // 2
    channels = lanes // zl
    column = lambda k: jnp.concatenate([x[:, 2 * k, :], x[:, 2 * k + 1, :]], axis=0)
    block = triple(jnp.concatenate([column(k) for k in range(kl)], axis=1))
    inner = lax.broadcasted_iota(jnp.int32, (1, kl * lanes), 1) % zl
    modes = jnp.zeros((forward.shape[1], kl * lanes), F32)
    for z in range(zl):
        modes += jnp.where(inner == z, dot(forward[z], block), 0.0)
    count = modes.shape[0] // 2
    modes = jnp.concatenate(
        [
            modes[p * count : (p + 1) * count, k * lanes : (k + 1) * lanes]
            for p in range(2)
            for k in range(kl)
        ],
        axis=0,
    )
    outs = channels * HALVES
    pairs = channels * outs
    lane = lax.broadcasted_iota(jnp.int32, (lanes, pairs), 0) // zl
    both = lax.broadcasted_iota(jnp.int32, (lanes, pairs), 1)
    spread = jnp.where(lane == both // outs, 1.0, 0.0).astype(BF)
    mh, ml = halves(modes)
    wide = dot(mh, spread) + dot(ml, spread)
    half = wide.shape[0] // 2
    re, im = wide[:half], wide[half:]
    wr = w[0, :, h * pairs : (h + 1) * pairs].astype(F32)
    wi = w[1, :, h * pairs : (h + 1) * pairs].astype(F32)
    mixed = jnp.concatenate([wr * re - wi * im, wr * im + wi * re], axis=0)
    both = lax.broadcasted_iota(jnp.int32, (pairs, outs * zl), 0)
    lane = lax.broadcasted_iota(jnp.int32, (pairs, outs * zl), 1) // zl
    gather = jnp.where(both % outs == lane, 1.0, 0.0).astype(BF)
    ph, plo = halves(mixed)
    return dot(ph, gather) + dot(plo, gather)


def bypass_rows(zl, h, w, bias):
    channels = w.shape[0]
    outs = channels // HALVES

    def picks(rows, first):
        row = lax.broadcasted_iota(jnp.int32, (rows * zl, channels), 0) // zl + first
        return row == lax.broadcasted_iota(jnp.int32, (rows * zl, channels), 1)

    pick = picks(outs, h * outs)
    ones = lambda p: jnp.where(p, 1.0, 0.0).astype(BF)
    left = dot(ones(pick), w[...], ((1,), (1,))).astype(BF)
    full = dot(left, ones(picks(channels, 0)), ((1,), (1,)))
    a = lax.broadcasted_iota(jnp.int32, full.shape, 0) % zl
    b = lax.broadcasted_iota(jnp.int32, full.shape, 1) % zl
    column = jnp.sum(jnp.where(pick, bias[...], 0.0), axis=1, keepdims=True)
    return jnp.where(a == b, full, 0.0).astype(BF), column


def field_rows(zl, spectrum, plane, mix, column, th, tl):
    high, low = halves(spectrum)
    first = ((0,), (0,))
    value = dot(jnp.concatenate([high, low], 0), th, first) + dot(high, tl, first)
    value = value + dot(mix, plane) + column
    return jax.nn.gelu(value).reshape(-1, zl, value.shape[1])


def spectrum_kernel(n_y, n_z, zl, *refs):
    (
        f_hbm, xt_hbm, yt_hbm, yi_hbm, zf_hbm, zi_hbm, w_hbm, th_hbm, tl_hbm, bypass, bias,
        r_hbm, o_hbm,
        f, xt, yt, yi, zf, zi, w, th, tl, mix, shift, a, theirs, summing, arrived, total, seen,
        mixed, back, ring, leaving, keeping, mine, done,
        load_sem, swap_s, swap_r, sum_s, sum_r, out_s, out_r, in_s, in_r, ring_s, ring_r,
        turn_s, turn_r, keep_s, done_s,
    ) = refs
    here, column = lax.axis_index("py"), lax.axis_index("pz")
    n_ring = n_y // 2
    side, z = here // n_ring, here % n_ring
    other = 1 - side
    half_py = lambda s, at: s * n_ring + at % n_ring
    partner = {"py": half_py(other, z)}
    neighbours = ({"py": half_py(side, z + 1)}, {"py": half_py(side, z + n_ring - 1)})

    barrier = pltpu.get_barrier_semaphore()
    for peer in (partner,) + neighbours:
        pl.semaphore_signal(barrier, inc=1, device_id=peer, device_id_type=MESH)

    def greet(step, carry):
        pl.semaphore_signal(
            barrier, inc=1, device_id={"pz": (column + step) % n_z}, device_id_type=MESH
        )
        return carry

    loads = []

    def load(source, target):
        copy = pltpu.make_async_copy(source, target, load_sem.at[len(loads)])
        copy.start()
        loads.append(copy)
        return copy

    pieces = 2
    rows = f.shape[1] // pieces
    channels = f.shape[0] // HALVES
    table_x = load(xt_hbm, xt)
    fields = []
    for h in range(HALVES):
        for i in range(pieces):
            at = (pl.ds(h * channels, channels), pl.ds(i * rows, rows), slice(None))
            fields.append(load(f_hbm.at[at], f.at[at]))
    depth = yt_hbm.shape[3]
    table_y = [
        load(yt_hbm.at[half_py(s, z)], yt.at[:, :, pl.ds(i * depth, depth)])
        for i, s in enumerate((side, other))
    ]
    table_z = [load(zf_hbm, zf), load(w_hbm, w)]
    table_b = [load(zi_hbm, zi)]
    table_i = [load(yi_hbm.at[half_py(s, z)], yi.at[i]) for i, s in enumerate((side, other))]
    table_f = [load(th_hbm, th), load(tl_hbm, tl)]
    lax.fori_loop(1, n_z, greet, 0)

    reach = n_ring // 2
    offsets = [reach] + [o * s for o in range(reach - 1, 0, -1) for s in (1, -1)] + [0]

    def swap(h, i):
        at = (z + offsets[i] + n_ring) % n_ring
        return pltpu.make_async_remote_copy(
            src_ref=a.at[h, half_py(other, at)],
            dst_ref=theirs.at[h, at],
            send_sem=swap_s.at[h * n_ring + i],
            recv_sem=swap_r.at[h * n_ring + i],
            device_id=partner,
            device_id_type=MESH,
        )

    table_x.wait()
    turns = f.shape[1] // (2 * zl) // pieces
    for h in range(HALVES):
        for i in range(pieces):
            fields[h * pieces + i].wait()
            x_forward(zl, f, xt, a, h, i * turns, (i + 1) * turns)
        if h == 0:
            pl.semaphore_wait(barrier, n_z + 2)
        for i in range(n_ring):
            swap(h, i).start()
    for copy in table_y:
        copy.wait()

    def partial(h, i):
        at = (z + offsets[i] + n_ring) % n_ring
        swap(h, i).wait_recv()
        block = jnp.concatenate([a[h, half_py(side, at)], theirs[h, at]], axis=0)
        high, low = halves(block)
        return dot3(yt[0], yt[1], high, low)

    part = total.shape[1] * total.shape[2] // GROUP
    span = lambda g: pl.ds(g * part, part)
    carries = lambda way, step, g: step > 0 or (g < GROUP // 2) == (way == 0)

    def hop(h, way, step, g):
        index = ((h * 2 + way) * reach + step) * GROUP + g
        return pltpu.make_async_remote_copy(
            src_ref=summing.at[h, way, step, span(g)],
            dst_ref=arrived.at[h, way, step, span(g)],
            send_sem=sum_s.at[index],
            recv_sem=sum_r.at[index],
            device_id=neighbours[way],
            device_id_type=MESH,
        )

    def set_out(h):
        block = partial(h, 0)
        for g in range(GROUP):
            way = 0 if g < GROUP // 2 else 1
            summing[h, way, 0, g * part : (g + 1) * part] = block[g * part : (g + 1) * part]
            hop(h, way, 0, g).start()

    def move_on(h, step):
        for way in range(2):
            summing[h, way, step] = partial(h, 2 * step - 1 + way)
        for g in range(GROUP):
            for way in range(2):
                if carries(way, step - 1, g):
                    hop(h, way, step - 1, g).wait_recv()
                    summing[h, way, step, span(g)] += arrived[h, way, step - 1, span(g)]
                hop(h, way, step, g).start()

    per = n_z // GROUP
    y_chip, place = column // GROUP, column % GROUP
    slot = place * per + y_chip

    def to_owner(h, source, owner, target):
        return pltpu.make_async_remote_copy(
            src_ref=total.at[h, source],
            dst_ref=seen.at[h, target],
            send_sem=out_s.at[h * n_z + owner],
            recv_sem=out_r.at[h * n_z + target],
            device_id={"pz": owner},
            device_id_type=MESH,
        )

    def arrive(h):
        last = partial(h, n_ring - 1)
        for g in range(GROUP):
            for way in range(2):
                hop(h, way, reach - 1, g).wait_recv()
            value = last[g * part : (g + 1) * part] + arrived[h, 0, reach - 1, span(g)]
            value = value + arrived[h, 1, reach - 1, span(g)]
            total[h, g * per : (g + 1) * per] = value.reshape((per,) + total.shape[2:])

            def send(i, carry):
                chip = (y_chip + i) % per
                owner = chip * GROUP + g

                @pl.when(owner != column)
                def _():
                    to_owner(h, g * per + chip, owner, column).start()

                return carry

            lax.fori_loop(0, per, send, 0)
        seen[h, column] = total[h, slot]

    def collect(h):
        def one(step, carry):
            peer = (column + step) % n_z
            to_owner(h, 0, peer, peer).wait()
            return carry

        lax.fori_loop(1, n_z, one, 0)

    set_out(0)
    for step in range(1, reach):
        move_on(0, step)
    set_out(1)
    arrive(0)
    for step in range(1, reach):
        move_on(1, step)
    for copy in table_z:
        copy.wait()
    collect(0)
    summed = mix_modes(zl, seen.at[0], w, zf, 0)
    arrive(1)
    rows_mix, rows_bias = bypass_rows(zl, 0, bypass, bias)
    mix[...] = rows_mix
    shift[...] = jnp.broadcast_to(rows_bias, shift.shape)
    for copy in table_b:
        copy.wait()
    collect(1)
    summed = summed + mix_modes(zl, seen.at[1], w, zf, 1)

    lanes = seen.shape[3]
    kl = seen.shape[2] // 2
    count = summed.shape[0] // (2 * kl)
    inner = lax.broadcasted_iota(jnp.int32, (1, kl * lanes), 1) % zl

    def to_cells(h, source, peer, target, sender):
        return pltpu.make_async_remote_copy(
            src_ref=mixed.at[h, source],
            dst_ref=back.at[h, target],
            send_sem=in_s.at[h * n_z + peer],
            recv_sem=in_r.at[h * n_z + sender],
            device_id={"pz": peer},
            device_id_type=MESH,
        )

    for h in range(HALVES):
        row = lambda p, k: summed[
            (p * kl + k) * count : (p * kl + k + 1) * count, h * lanes : (h + 1) * lanes
        ]
        columns = [jnp.concatenate([row(0, k), row(1, k)], axis=0) for k in range(kl)]
        modes = triple(jnp.concatenate(columns, axis=1))
        for g in range(GROUP):
            value = dot(zi[g], modes)
            size = 2 * per
            cells = jnp.zeros((size, modes.shape[1]), F32)
            for i in range(zl):
                cells += jnp.where(inner == i, value[i * size : (i + 1) * size], 0.0)
            for p in range(2):
                for k in range(kl):
                    mixed[h, g * per : (g + 1) * per, 2 * k + p, :] = cells[
                        p * per : (p + 1) * per, k * lanes : (k + 1) * lanes
                    ]

            def send_back(i, carry):
                chip = (y_chip + i) % per
                peer = chip * GROUP + g

                @pl.when(peer != column)
                def _():
                    to_cells(h, g * per + chip, peer, slot, column).start()

                return carry

            lax.fori_loop(0, per, send_back, 0)
        back[h, slot] = mixed[h, slot]

    def end_back(h):
        def one(step, carry):
            peer = (column + step) % n_z
            to_cells(h, 0, peer, 0, peer).wait()
            return carry

        lax.fori_loop(1, n_z, one, 0)

    wide = lambda g: pl.ds(g * per, per)
    passes = lambda way, step, g: step < reach - 1 or (g < GROUP // 2) == (way == 0)

    def relay(h, way, step, g):
        index = ((h * 2 + way) * reach + step) * GROUP + g
        source = back.at[h, wide(g)] if step == 0 else ring.at[h, way, step - 1, wide(g)]
        target = ring.at[h, 0 if step == reach - 1 else way, step, wide(g)]
        return pltpu.make_async_remote_copy(
            src_ref=source,
            dst_ref=target,
            send_sem=ring_s.at[index],
            recv_sem=ring_r.at[index],
            device_id=neighbours[way],
            device_id_type=MESH,
        )

    def turn(h, i, owner):
        return pltpu.make_async_remote_copy(
            src_ref=leaving.at[h, i],
            dst_ref=(mine if h == 0 else r_hbm).at[owner],
            send_sem=turn_s.at[h * n_ring + i],
            recv_sem=turn_r.at[h * n_ring + i],
            device_id=partner,
            device_id_type=MESH,
        )

    def keep(i, owner):
        return pltpu.make_async_copy(keeping.at[i], r_hbm.at[owner], keep_s.at[i])

    def spread(h, i, offset, block):
        owner = half_py(side, z + offset + n_ring)
        high, low = halves(block.reshape(-1, block.shape[2]))
        leaving[h, i] = dot3(yi[1, 0], yi[1, 1], high, low)
        turn(h, i, owner).start()
        own = dot3(yi[0, 0], yi[0, 1], high, low)
        if h == 0:
            mine[owner] = own
        else:
            keeping[i] = own
            keep(i, owner).start()

    def send_own(h):
        for g in range(GROUP):
            for way in range(2):
                relay(h, way, 0, g).start()

    def pass_on(h, step):
        for g in range(GROUP):
            for way in range(2):
                if passes(way, step - 1, g):
                    relay(h, way, step - 1, g).wait_recv()
                if step < reach and passes(way, step, g):
                    relay(h, way, step, g).start()

    def spread_pair(h, step):
        if step == reach:
            spread(h, n_ring - 1, reach, ring[h, 0, reach - 1])
        else:
            for way in range(2):
                spread(h, 2 * step - 1 + way, step if way else -step, ring[h, way, step - 1])

    strip = f.shape[1] // reach
    strip_at = lambda i: (slice(None), pl.ds(i * strip, strip), slice(None))

    def finished(i):
        return pltpu.make_async_copy(done.at[strip_at(i)], o_hbm.at[strip_at(i)], done_s.at[i])

    def finish(number):
        def one(i, carry):
            at = pl.ds(pl.multiple_of(i * 2 * zl, 2 * zl), 2 * zl)
            block = f[:, at, :].astype(F32)
            made = []
            for y in range(2):
                plane = block[:, y * zl : (y + 1) * zl, :].reshape(-1, block.shape[2]).astype(BF)
                depth = leaving.shape[2] * zl // f.shape[1]
                start = pl.multiple_of((i * 2 + y) * depth, depth)
                values = mine[:, pl.ds(start, depth), :].reshape(-1, lanes)
                made.append(field_rows(zl, values, plane, mix[...], shift[...], th[...], tl[...]))
            done[:, at, :] = jnp.concatenate(made, axis=1).astype(BF)
            return carry

        each = strip // (2 * zl)
        lax.fori_loop(number * each, (number + 1) * each, one, 0)
        finished(number).start()

    for copy in table_i:
        copy.wait()
    end_back(0)
    send_own(0)
    spread(0, 0, 0, back[0])
    end_back(1)
    spread(1, 0, 0, back[1])
    pass_on(0, 1)
    send_own(1)
    spread_pair(0, 1)
    pass_on(0, 2)
    spread_pair(0, 2)
    pass_on(1, 1)
    for step in range(3, reach):
        pass_on(0, step)
        spread_pair(0, step)
    pass_on(0, reach)
    spread_pair(0, reach)
    spread_pair(1, 1)
    pass_on(1, 2)
    spread_pair(1, 2)
    for copy in table_f:
        copy.wait()
    for i in range(n_ring):
        turn(0, i, here).wait_recv()
    finish(0)
    for step in range(3, reach):
        pass_on(1, step)
        spread_pair(1, step)
    finish(1)
    pass_on(1, reach)
    spread_pair(1, reach)
    for i in range(2, reach):
        finish(i)

    for h in range(HALVES):
        for i in range(n_ring):
            swap(h, i).wait_send()
        for step in range(reach):
            for g in range(GROUP):
                for way in range(2):
                    if carries(way, step, g):
                        hop(h, way, step, g).wait_send()
                    if passes(way, step, g):
                        relay(h, way, step, g).wait_send()
    for i in range(n_ring):
        turn(0, i, here).wait_send()
        keep(i, here).wait()
        turn(1, i, here).wait()
    for i in range(reach):
        finished(i).wait()


def field_kernel(zl, r_ref, f_ref, o_first, w_ref, b_ref, th_ref, tl_ref, o_ref, mix, shift):
    @pl.when(pl.program_id(0) == 0)
    def _():
        rows_mix, rows_bias = bypass_rows(zl, 1, w_ref, b_ref)
        mix[...] = rows_mix
        shift[...] = jnp.broadcast_to(rows_bias, shift.shape)

    outs = o_first.shape[0]
    o_ref[:outs] = o_first[...]
    block = f_ref[...].astype(F32)
    for y in range(f_ref.shape[1] // zl):
        plane = block[:, y * zl : (y + 1) * zl, :].reshape(-1, block.shape[2]).astype(BF)
        values = r_ref[:, y].reshape(-1, r_ref.shape[3])
        made = field_rows(zl, values, plane, mix[...], shift[...], th_ref[...], tl_ref[...])
        o_ref[outs:, y * zl : (y + 1) * zl, :] = made.astype(BF)


def whole(shape):
    return pl.BlockSpec(shape, lambda i: (0,) * len(shape))


def per_device(tables, n_y, n_z, features, spectral_weight, bypass_weight, bias_vector):
    xf, xi, yf, yi, zf, zi = tables
    c, yl, zl, nx = features.shape
    _, kl, _, mz, pairs = spectral_weight.shape
    outs = c // HALVES
    lanes = outs * zl
    part = 2 * kl
    rows = yl * part
    flat = features.reshape(c, yl * zl, nx)
    x_rows = split(xf).reshape(-1, nx)
    y_rows, y_back = split(yf, 1), split(yi, 1)
    z_rows, z_back = thrice(zf), thrice(zi)
    high, tl = split(xi)
    th = np.concatenate([high, high], 0)
    weight = spectral_weight.reshape(2, kl * mz, pairs)
    bias = bias_vector.reshape(1, c)
    my_rows = y_rows.shape[2]
    modes = my_rows // part
    n_ring = n_y // 2
    reach = n_ring // 2
    th, tl = jnp.asarray(th), jnp.asarray(tl)
    operands = [flat] + [jnp.asarray(t) for t in (x_rows, y_rows, y_back, z_rows, z_back)]
    operands += [weight, th, tl]
    hops = HALVES * 2 * reach * GROUP
    sems = [20] + [HALVES * n_ring] * 2 + [hops] * 2 + [HALVES * n_z] * 4 + [hops] * 2
    sems += [HALVES * n_ring] * 2 + [n_ring, reach]
    planes, ready = pl.pallas_call(
        functools.partial(spectrum_kernel, n_y, n_z, zl),
        out_shape=(
            jax.ShapeDtypeStruct((n_y, rows, lanes), F32),
            jax.ShapeDtypeStruct((outs, yl * zl, nx), BF),
        ),
        in_specs=[pl.BlockSpec(memory_space=pl.ANY)] * len(operands)
        + [pl.BlockSpec(memory_space=pltpu.VMEM)] * 2,
        out_specs=(pl.BlockSpec(memory_space=pl.ANY), pl.BlockSpec(memory_space=pl.ANY)),
        scratch_shapes=[
            pltpu.VMEM(flat.shape, BF),
            pltpu.VMEM(x_rows.shape, BF),
            pltpu.VMEM((2, my_rows, 2 * rows), BF),
            pltpu.VMEM((2,) + y_back.shape[1:], BF),
            pltpu.VMEM(z_rows.shape, BF),
            pltpu.VMEM(z_back.shape, BF),
            pltpu.VMEM(weight.shape, BF),
            pltpu.VMEM(th.shape, BF),
            pltpu.VMEM(tl.shape, BF),
            pltpu.VMEM((lanes, c * zl), BF),
            pltpu.VMEM((lanes, nx), F32),
            pltpu.VMEM((HALVES, n_y, rows, lanes), F32),
            pltpu.VMEM((HALVES, n_ring, rows, lanes), F32),
            pltpu.VMEM((HALVES, 2, reach, my_rows, lanes), F32),
            pltpu.VMEM((HALVES, 2, reach, my_rows, lanes), F32),
            pltpu.VMEM((HALVES, modes, part, lanes), F32),
            pltpu.VMEM((HALVES, n_z, part, lanes), F32),
            pltpu.VMEM((HALVES, n_z, part, lanes), F32),
            pltpu.VMEM((HALVES, modes, part, lanes), F32),
            pltpu.VMEM((HALVES, 2, reach, modes, part, lanes), F32),
            pltpu.VMEM((HALVES, n_ring, rows, lanes), F32),
            pltpu.VMEM((n_ring, rows, lanes), F32),
            pltpu.VMEM((n_y, rows, lanes), F32),
            pltpu.VMEM((outs, yl * zl, nx), BF),
        ]
        + [pltpu.SemaphoreType.DMA((n,)) for n in sems],
        compiler_params=pltpu.CompilerParams(
            collective_id=0, has_side_effects=True, vmem_limit_bytes=62 * MIB
        ),
        name="spectrum",
    )(*operands, bypass_weight, bias)

    step = 4
    block = lambda count: pl.BlockSpec((count, step * zl, nx), lambda i: (0, i, 0))
    out = pl.pallas_call(
        functools.partial(field_kernel, zl),
        grid=(yl // step,),
        in_specs=[
            pl.BlockSpec((n_y, step, part, lanes), lambda i: (0, i, 0, 0)),
            block(c),
            block(outs),
            whole(bypass_weight.shape),
            whole(bias.shape),
            whole(th.shape),
            whole(tl.shape),
        ],
        out_specs=block(c),
        out_shape=jax.ShapeDtypeStruct(flat.shape, BF),
        scratch_shapes=[pltpu.VMEM((lanes, c * zl), BF), pltpu.VMEM((lanes, nx), F32)],
        compiler_params=pltpu.CompilerParams(vmem_limit_bytes=62 * MIB),
        name="field",
    )(planes.reshape(n_y, yl, part, lanes), flat, ready, bypass_weight, bias, th, tl)
    return out.reshape(features.shape)


def solution(mesh):
    n_y, n_z = mesh.shape["py"], mesh.shape["pz"]

    def run(features, spectral_weight, bypass_weight, bias_vector):
        _, ny, nz, nx = features.shape
        _, mx, my, mz, _ = spectral_weight.shape
        tables = make_tables(nx, ny, nz, mx, my, mz, n_y, n_z)
        return jax.shard_map(
            functools.partial(per_device, tables, n_y, n_z),
            mesh=mesh,
            in_specs=(P(None, "py", "pz", None), P(None, "py", "pz", None, None), P(), P()),
            out_specs=P(None, "py", "pz", None),
            check_vma=False,
        )(features, spectral_weight, bypass_weight, bias_vector)

    return run
```

time: 103 us -> 107 us (1.039)
  Pallas kernels: 102 us -> 106 us
    pallas_call x1, Pallas kernels: 95.6 us -> 101 us  [per_device(): pl.pallas_call(functools.partial(spectrum_kernel, n_y, n_z, zl), out_shap...]
    pallas_call x1, Pallas kernels: 6.45 us -> 5.34 us  [per_device(): pl.pallas_call(functools.partial(field_kernel, zl), grid=(yl // step,), i...]
where the time goes in v4:
time: 107 us; the launch traced here: 106 us
  Pallas kernels  106 us (99%)
    pallas_call x1, Pallas kernels, per_device(): pl.pallas_call(functools.partial(spectrum_kernel, n_y, n_z, zl), out_shap...  101 us
    pallas_call x1, Pallas kernels, per_device(): pl.pallas_call(functools.partial(field_kernel, zl), grid=(yl // step,), i...  5.34 us

profile of v4, /device:TPU:6, one launch (start us, length us, event | category | flops | bytes accessed | tf_op | source)
XLA Modules:
  0.0 106.1 jit_solution(2562398690339452361)
XLA Ops:
  0.0 100.7 %spectrum.1 = (f32[16,128,128]{2,1,0:T(8,128)}, bf16[16,128,256]{2,1,0:T(8,128)(2,1)}) custom-call(bf16[32,128,256]{2,1,0:T(8,128)(2,1)} %bitcast.5, bf16[256,256]{1,0:T(8,128)(2,1)} %constant.16.clone.refs_1_, bf16[16,2,256,128]{3,2,1,0:T(8,128)(2,1)} %constant.17.clone.refs_2_, bf16[16,2,128,256]{3,2,1,0:T(8,128)(2,1)} %constant.18.clone.refs_3_, ...), custom_call_target="tpu_custom_call" | custom-call | tf_op jit(solution)/shard_map/spectrum/pallas_call | solution.py:591
  100.7 5.3 %field.1 = bf16[32,128,256]{2,1,0:T(8,128)(2,1)} custom-call(f32[16,16,8,128]{3,2,1,0:T(8,128)} %bitcast.7, bf16[32,128,256]{2,1,0:T(8,128)(2,1)} %bitcast.6, bf16[16,128,256]{2,1,0:T(8,128)(2,1)} %get-tuple-element.8.o_first, bf16[32,32]{1,0:T(8,128)(2,1)} %w_ref.1, f32[1,32]{1,0:T(1,128)} %bitcast.10, bf16[256,256]{1,0:T(8,128)(2,1)} %constant.14.clone.refs_7_.th_ref, ...), custom_call_target="tpu_custom_call" | custom-call | tf_op jit(solution)/shard_map/field/pallas_call | solution.py:635

commit v5 on v4

v5 whole, which is shorter than its diff:
```python
import functools
import math

import jax
import jax.numpy as jnp
import ml_dtypes
import numpy as np
from jax import lax
from jax.experimental import pallas as pl
from jax.experimental.pallas import tpu as pltpu
from jax.sharding import PartitionSpec as P

MESH = pl.DeviceIdType.MESH
BF = jnp.bfloat16
F32 = jnp.float32
MIB = 1 << 20
PARTS = 2
LH = 2
GROUP = 4


def centred(count):
    index = np.arange(count)
    return np.where(index < count // 2, index, index - count)


def split(table, axis=0):
    high = table.astype(ml_dtypes.bfloat16)
    low = (table - high.astype(np.float64)).astype(ml_dtypes.bfloat16)
    return np.stack([high, low], axis)


def thrice(table):
    high, low = split(table)
    return np.concatenate([high, high, low], -1)


def pair(frequencies, positions, period, sign):
    angle = 2.0 * np.pi * ((positions[:, None] * frequencies[None, :]) % period) / period
    c, s = np.cos(angle), np.sin(angle)
    return np.stack([np.stack([c, sign * s]), np.stack([-sign * s, c])])


def make_tables(nx, ny, nz, mx, my, mz, py, pz):
    k = mx // py
    zl = nz // pz
    yl = ny // py
    norm = 1.0 / math.sqrt(nx * ny * nz)
    angle = 2.0 * np.pi * ((np.arange(mx)[:, None] * np.arange(nx)[None, :]) % nx) / nx
    kp = k // PARTS
    eye, pairs = np.eye(kp), np.eye(2)
    xf = np.stack([np.cos(angle) * norm, -np.sin(angle) * norm], 1)
    xf = xf.reshape(py, PARTS, kp, 2, nx)
    xf = np.einsum("dtkpx,yw->tdykpwx", xf, pairs).reshape(PARTS, py * 4 * kp, 2 * nx)
    weight = np.where(np.arange(mx) == 0, 1.0, 2.0)[:, None] * norm
    xi = np.stack([np.cos(angle) * weight, -np.sin(angle) * weight], 1)
    xi = xi.reshape(py, PARTS, kp, 2, nx).swapaxes(0, 1).reshape(2 * mx, nx)
    order = np.arange(my).reshape(pz // GROUP, GROUP).T.reshape(-1)
    yf = pair(centred(my), np.arange(ny), ny, -1.0)[..., order].reshape(2, 2, py, yl, my)
    yf = np.einsum("pqdyj,kl,hg->djhkqgylp", yf, eye, pairs)
    yf = yf.reshape(py, my * 4 * kp, yl * 4 * kp)
    yi = pair(centred(my), np.arange(ny), ny, 1.0)[..., order].reshape(2, 2, py, yl, my)
    yi = np.einsum("qrdyj,kl,hg->dhkryjglq", yi, eye, pairs)
    yi = yi.reshape(py, yl * 4 * kp, my * 4 * kp)
    zf = pair(centred(mz), np.arange(nz), nz, -1.0).reshape(2, 2, pz, zl, mz)
    zf = np.einsum("pqszm->zqmps", zf).reshape(zl, 2 * mz, 2 * pz)
    zi = pair(centred(mz), np.arange(nz), nz, 1.0).reshape(2, 2, pz // GROUP, GROUP, zl, mz)
    zi = np.einsum("qrjgzm->gzrjqm", zi).reshape(GROUP, zl * 2 * pz // GROUP, 2 * mz)
    return xf, xi, yf, yi, zf, zi


def halves(value):
    high = value.astype(BF)
    return high, (value - high.astype(F32)).astype(BF)


def triple(value):
    high, low = halves(value)
    return jnp.concatenate([high, low, high], 0)


def dot(a, b, dims=((1,), (0,))):
    return lax.dot_general(a, b, (dims, ((), ())), preferred_element_type=F32)


def dot3(ah, al, bh, bl):
    return dot(ah, bh) + dot(al, bh) + dot(ah, bl)


def x_forward(zl, field, table, out, t, first, last):
    length = field.shape[2]

    def step(i, carry):
        block = field[:, pl.ds(pl.multiple_of(i * 2 * zl, 2 * zl), 2 * zl), :].astype(F32)
        both = None
        for y in range(2):
            plane = block[:, y * zl : (y + 1) * zl, :].reshape(-1, length).astype(BF)
            term = dot(table[t, :, y * length : (y + 1) * length], plane, ((1,), (1,)))
            both = term if both is None else both + term
        half = both.shape[0] // 2
        rows = half // out.shape[1]
        out[t, :, pl.ds(pl.multiple_of(i * rows, rows), rows), :] = (
            both[:half] + both[half:]
        ).reshape(out.shape[1], rows, out.shape[3])
        return carry

    lax.fori_loop(first, last, step, 0)


def mix_modes(zl, x, w, forward, t):
    cells, rows, tile = x.shape
    lanes = LH * tile
    kp = rows // (2 * LH)
    channels = lanes // zl
    row = lambda k, q: jnp.concatenate([x[:, (h * kp + k) * 2 + q, :] for h in range(LH)], axis=1)
    column = lambda k: jnp.concatenate([row(k, 0), row(k, 1)], axis=0)
    block = triple(jnp.concatenate([column(k) for k in range(kp)], axis=1))
    inner = lax.broadcasted_iota(jnp.int32, (1, kp * lanes), 1) % zl
    modes = jnp.zeros((forward.shape[1], kp * lanes), F32)
    for z in range(zl):
        modes += jnp.where(inner == z, dot(forward[z], block), 0.0)
    count = modes.shape[0] // 2
    modes = jnp.concatenate(
        [
            modes[p * count : (p + 1) * count, k * lanes : (k + 1) * lanes]
            for p in range(2)
            for k in range(kp)
        ],
        axis=0,
    )
    pairs = w.shape[2]
    lane = lax.broadcasted_iota(jnp.int32, (lanes, pairs), 0) // zl
    both = lax.broadcasted_iota(jnp.int32, (lanes, pairs), 1)
    spread = jnp.where(lane == both // channels, 1.0, 0.0).astype(BF)
    mh, ml = halves(modes)
    wide = dot(mh, spread) + dot(ml, spread)
    half = wide.shape[0] // 2
    re, im = wide[:half], wide[half:]
    wr = w[0, t * half : (t + 1) * half, :].astype(F32)
    wi = w[1, t * half : (t + 1) * half, :].astype(F32)
    mixed = jnp.concatenate([wr * re - wi * im, wr * im + wi * re], axis=0)
    both = lax.broadcasted_iota(jnp.int32, (pairs, lanes), 0)
    lane = lax.broadcasted_iota(jnp.int32, (pairs, lanes), 1) // zl
    gather = jnp.where(both % channels == lane, 1.0, 0.0).astype(BF)
    ph, plo = halves(mixed)
    summed = dot(ph, gather) + dot(plo, gather)
    part = lambda p, k: summed[(p * kp + k) * count : (p * kp + k + 1) * count]
    columns = [jnp.concatenate([part(0, k), part(1, k)], axis=0) for k in range(kp)]
    return triple(jnp.concatenate(columns, axis=1))


def bypass_rows(zl, w, bias):
    channels = w.shape[0]
    row = lax.broadcasted_iota(jnp.int32, (channels * zl, channels), 0) // zl
    pick = row == lax.broadcasted_iota(jnp.int32, (channels * zl, channels), 1)
    ones = jnp.where(pick, 1.0, 0.0).astype(BF)
    left = dot(ones, w[...], ((1,), (1,))).astype(BF)
    full = dot(left, ones, ((1,), (1,)))
    a = lax.broadcasted_iota(jnp.int32, full.shape, 0) % zl
    b = lax.broadcasted_iota(jnp.int32, full.shape, 1) % zl
    column = jnp.sum(jnp.where(pick, bias[...], 0.0), axis=1, keepdims=True)
    return jnp.where(a == b, full, 0.0).astype(BF), column


def field_rows(zl, spectrum, plane, mix, column, th, tl):
    high, low = halves(spectrum)
    first = ((0,), (0,))
    value = dot(jnp.concatenate([high, low], 0), th, first) + dot(high, tl, first)
    value = value + dot(mix, plane) + column
    return jax.nn.gelu(value).reshape(-1, zl, value.shape[1])


def spectrum_kernel(n_y, n_z, zl, *refs):
    (
        f_hbm, xt_hbm, yt_hbm, yi_hbm, zf_hbm, zi_hbm, w_hbm, r_hbm,
        f, xt, yt, yi, zf, zi, w, a, theirs, summing, arrived, total, seen,
        mixed, back, ring, leaving, keeping,
        load_sem, swap_s, swap_r, sum_s, sum_r, out_s, out_r, in_s, in_r, ring_s, ring_r,
        turn_s, turn_r, keep_s,
    ) = refs
    here, column = lax.axis_index("py"), lax.axis_index("pz")
    n_ring = n_y // 2
    side, z = here // n_ring, here % n_ring
    other = 1 - side
    half_py = lambda s, at: s * n_ring + at % n_ring
    partner = {"py": half_py(other, z)}
    neighbours = ({"py": half_py(side, z + 1)}, {"py": half_py(side, z + n_ring - 1)})

    barrier = pltpu.get_barrier_semaphore()
    for peer in (partner,) + neighbours:
        pl.semaphore_signal(barrier, inc=1, device_id=peer, device_id_type=MESH)

    def greet(step, carry):
        pl.semaphore_signal(
            barrier, inc=1, device_id={"pz": (column + step) % n_z}, device_id_type=MESH
        )
        return carry

    loads = []

    def load(source, target):
        copy = pltpu.make_async_copy(source, target, load_sem.at[len(loads)])
        copy.start()
        loads.append(copy)
        return copy

    pieces = 4
    rows = f.shape[1] // pieces
    table_x = load(xt_hbm, xt)
    fields = [
        load(f_hbm.at[:, pl.ds(i * rows, rows), :], f.at[:, pl.ds(i * rows, rows), :])
        for i in range(pieces)
    ]
    depth = yt_hbm.shape[3]
    table_y = [
        load(yt_hbm.at[half_py(s, z)], yt.at[:, :, pl.ds(i * depth, depth)])
        for i, s in enumerate((side, other))
    ]
    table_z = [load(zf_hbm, zf), load(w_hbm, w), load(zi_hbm, zi)]
    table_i = [load(yi_hbm.at[half_py(s, z)], yi.at[i]) for i, s in enumerate((side, other))]
    lax.fori_loop(1, n_z, greet, 0)

    reach = n_ring // 2
    offsets = [reach] + [o * s for o in range(reach - 1, 0, -1) for s in (1, -1)] + [0]

    def swap(h, i):
        at = (z + offsets[i] + n_ring) % n_ring
        return pltpu.make_async_remote_copy(
            src_ref=a.at[h, half_py(other, at)],
            dst_ref=theirs.at[h, at],
            send_sem=swap_s.at[h * n_ring + i],
            recv_sem=swap_r.at[h * n_ring + i],
            device_id=partner,
            device_id_type=MESH,
        )

    table_x.wait()
    turns = f.shape[1] // (2 * zl) // pieces
    for h in range(PARTS):
        for i in range(pieces):
            if h == 0:
                fields[i].wait()
            x_forward(zl, f, xt, a, h, i * turns, (i + 1) * turns)
        if h == 0:
            pl.semaphore_wait(barrier, n_z + 2)
        for i in range(n_ring):
            swap(h, i).start()
    for copy in table_y:
        copy.wait()

    def partial(h, i):
        at = (z + offsets[i] + n_ring) % n_ring
        swap(h, i).wait_recv()
        rows = (a[h, half_py(side, at)], theirs[h, at])
        tile = summing.shape[4]
        block = jnp.concatenate(
            [r[:, i * tile : (i + 1) * tile] for r in rows for i in range(LH)], axis=0
        )
        high, low = halves(block)
        return dot3(yt[0], yt[1], high, low)

    part = total.shape[1] * total.shape[2] // GROUP
    span = lambda g: pl.ds(g * part, part)
    carries = lambda way, step, g: step > 0 or (g < GROUP // 2) == (way == 0)

    def hop(h, way, step, g):
        index = ((h * 2 + way) * reach + step) * GROUP + g
        return pltpu.make_async_remote_copy(
            src_ref=summing.at[h, way, step, span(g)],
            dst_ref=arrived.at[h, way, step, span(g)],
            send_sem=sum_s.at[index],
            recv_sem=sum_r.at[index],
            device_id=neighbours[way],
            device_id_type=MESH,
        )

    def set_out(h):
        block = partial(h, 0)
        for g in range(GROUP):
            way = 0 if g < GROUP // 2 else 1
            summing[h, way, 0, g * part : (g + 1) * part] = block[g * part : (g + 1) * part]
            hop(h, way, 0, g).start()

    def move_on(h, step):
        for way in range(2):
            summing[h, way, step] = partial(h, 2 * step - 1 + way)
        for g in range(GROUP):
            for way in range(2):
                if carries(way, step - 1, g):
                    hop(h, way, step - 1, g).wait_recv()
                    summing[h, way, step, span(g)] += arrived[h, way, step - 1, span(g)]
                hop(h, way, step, g).start()

    per = n_z // GROUP
    y_chip, place = column // GROUP, column % GROUP
    slot = place * per + y_chip

    def to_owner(h, source, owner, target):
        return pltpu.make_async_remote_copy(
            src_ref=total.at[h, source],
            dst_ref=seen.at[h, target],
            send_sem=out_s.at[h * n_z + owner],
            recv_sem=out_r.at[h * n_z + target],
            device_id={"pz": owner},
            device_id_type=MESH,
        )

    def arrive(h):
        last = partial(h, n_ring - 1)
        for g in range(GROUP):
            for way in range(2):
                hop(h, way, reach - 1, g).wait_recv()
            value = last[g * part : (g + 1) * part] + arrived[h, 0, reach - 1, span(g)]
            value = value + arrived[h, 1, reach - 1, span(g)]
            total[h, g * per : (g + 1) * per] = value.reshape((per,) + total.shape[2:])

            def send(i, carry):
                chip = (y_chip + i) % per
                owner = chip * GROUP + g

                @pl.when(owner != column)
                def _():
                    to_owner(h, g * per + chip, owner, column).start()

                return carry

            lax.fori_loop(0, per, send, 0)
        seen[h, column] = total[h, slot]

    def collect(h):
        def one(step, carry):
            peer = (column + step) % n_z
            to_owner(h, 0, peer, peer).wait()
            return carry

        lax.fori_loop(1, n_z, one, 0)

    def to_cells(h, source, peer, target, sender):
        return pltpu.make_async_remote_copy(
            src_ref=mixed.at[h, source],
            dst_ref=back.at[h, target],
            send_sem=in_s.at[h * n_z + peer],
            recv_sem=in_r.at[h * n_z + sender],
            device_id={"pz": peer},
            device_id_type=MESH,
        )

    tile = seen.shape[3]
    kp = seen.shape[2] // (2 * LH)
    lanes = LH * tile
    inner = lax.broadcasted_iota(jnp.int32, (1, kp * lanes), 1) % zl

    def mix_and_return(h):
        modes = mix_modes(zl, seen.at[h], w, zf, h)
        for g in range(GROUP):
            value = dot(zi[g], modes)
            size = 2 * per
            cells = jnp.zeros((size, modes.shape[1]), F32)
            for i in range(zl):
                cells += jnp.where(inner == i, value[i * size : (i + 1) * size], 0.0)
            for p in range(2):
                for k in range(kp):
                    for i in range(LH):
                        mixed[h, g * per : (g + 1) * per, (i * kp + k) * 2 + p, :] = cells[
                            p * per : (p + 1) * per,
                            k * lanes + i * tile : k * lanes + (i + 1) * tile,
                        ]

            def send_back(i, carry):
                chip = (y_chip + i) % per
                peer = chip * GROUP + g

                @pl.when(peer != column)
                def _():
                    to_cells(h, g * per + chip, peer, slot, column).start()

                return carry

            lax.fori_loop(0, per, send_back, 0)
        back[h, slot] = mixed[h, slot]

    def end_back(h):
        def one(step, carry):
            peer = (column + step) % n_z
            to_cells(h, 0, peer, 0, peer).wait()
            return carry

        lax.fori_loop(1, n_z, one, 0)

    wide = lambda g: pl.ds(g * per, per)
    passes = lambda way, step, g: step < reach - 1 or (g < GROUP // 2) == (way == 0)

    def relay(h, way, step, g):
        index = ((h * 2 + way) * reach + step) * GROUP + g
        source = back.at[h, wide(g)] if step == 0 else ring.at[h, way, step - 1, wide(g)]
        target = ring.at[h, 0 if step == reach - 1 else way, step, wide(g)]
        return pltpu.make_async_remote_copy(
            src_ref=source,
            dst_ref=target,
            send_sem=ring_s.at[index],
            recv_sem=ring_r.at[index],
            device_id=neighbours[way],
            device_id_type=MESH,
        )

    def turn(h, i, owner):
        return pltpu.make_async_remote_copy(
            src_ref=leaving.at[h, i],
            dst_ref=r_hbm.at[:, h, owner],
            send_sem=turn_s.at[h * n_ring + i],
            recv_sem=turn_r.at[h * n_ring + i],
            device_id=partner,
            device_id_type=MESH,
        )

    def keep(h, i, owner):
        return pltpu.make_async_copy(
            keeping.at[h, i], r_hbm.at[:, h, owner], keep_s.at[h * n_ring + i]
        )

    def spread(h, i, offset, block):
        owner = half_py(side, z + offset + n_ring)
        high, low = halves(block.reshape(-1, block.shape[2]))
        leaving[h, i] = dot3(yi[1, 0], yi[1, 1], high, low).reshape(leaving.shape[2:])
        turn(h, i, owner).start()
        keeping[h, i] = dot3(yi[0, 0], yi[0, 1], high, low).reshape(keeping.shape[2:])
        keep(h, i, owner).start()

    def send_own(h):
        for g in range(GROUP):
            for way in range(2):
                relay(h, way, 0, g).start()

    def pass_on(h, step):
        for g in range(GROUP):
            for way in range(2):
                if passes(way, step - 1, g):
                    relay(h, way, step - 1, g).wait_recv()
                if step < reach and passes(way, step, g):
                    relay(h, way, step, g).start()

    def spread_pair(h, step):
        if step == reach:
            spread(h, n_ring - 1, reach, ring[h, 0, reach - 1])
        else:
            for way in range(2):
                spread(h, 2 * step - 1 + way, step if way else -step, ring[h, way, step - 1])

    set_out(0)
    for step in range(1, reach):
        move_on(0, step)
    set_out(1)
    arrive(0)
    for step in range(1, reach):
        move_on(1, step)
    for copy in table_z:
        copy.wait()
    collect(0)
    mix_and_return(0)
    arrive(1)
    for copy in table_i:
        copy.wait()
    end_back(0)
    send_own(0)
    spread(0, 0, 0, back[0])
    collect(1)
    mix_and_return(1)
    for step in range(1, reach):
        pass_on(0, step)
        spread_pair(0, step)
    pass_on(0, reach)
    end_back(1)
    send_own(1)
    spread_pair(0, reach)
    spread(1, 0, 0, back[1])
    for step in range(1, reach + 1):
        pass_on(1, step)
        spread_pair(1, step)

    for h in range(PARTS):
        for i in range(n_ring):
            swap(h, i).wait_send()
            keep(h, i, here).wait()
            turn(h, i, here).wait()
        for step in range(reach):
            for g in range(GROUP):
                for way in range(2):
                    if carries(way, step, g):
                        hop(h, way, step, g).wait_send()
                    if passes(way, step, g):
                        relay(h, way, step, g).wait_send()


def field_kernel(zl, r_ref, f_ref, w_ref, b_ref, th_ref, tl_ref, o_ref, mix, shift):
    @pl.when(pl.program_id(0) == 0)
    def _():
        rows_mix, rows_bias = bypass_rows(zl, w_ref, b_ref)
        mix[...] = rows_mix
        shift[...] = jnp.broadcast_to(rows_bias, shift.shape)

    block = f_ref[...].astype(F32)
    for y in range(f_ref.shape[1] // zl):
        plane = block[:, y * zl : (y + 1) * zl, :].reshape(-1, block.shape[2]).astype(BF)
        values = jnp.concatenate([r_ref[i, :, y, :] for i in range(LH)], axis=1)
        made = field_rows(zl, values, plane, mix[...], shift[...], th_ref[...], tl_ref[...])
        o_ref[:, y * zl : (y + 1) * zl, :] = made.astype(BF)


def whole(shape):
    return pl.BlockSpec(shape, lambda i: (0,) * len(shape))


def per_device(tables, n_y, n_z, features, spectral_weight, bypass_weight, bias_vector):
    xf, xi, yf, yi, zf, zi = tables
    c, yl, zl, nx = features.shape
    _, kl, _, mz, pairs = spectral_weight.shape
    lanes = c * zl
    tile = lanes // LH
    kp = kl // PARTS
    rows = yl * 2 * kp
    part = LH * 2 * kp
    flat = features.reshape(c, yl * zl, nx)
    x_rows = split(xf, 1).reshape(PARTS, -1, 2 * nx)
    y_rows, y_back = split(yf, 1), split(yi, 1)
    z_rows, z_back = thrice(zf), thrice(zi)
    high, tl = split(xi)
    th = np.concatenate([high, high], 0)
    weight = spectral_weight.reshape(2, kl * mz, pairs)
    bias = bias_vector.reshape(1, c)
    my_rows = y_rows.shape[2]
    modes = my_rows // part
    n_ring = n_y // 2
    reach = n_ring // 2
    operands = [flat] + [jnp.asarray(t) for t in (x_rows, y_rows, y_back, z_rows, z_back)] + [weight]
    hops = PARTS * 2 * reach * GROUP
    turns = PARTS * n_ring
    sems = [16] + [turns] * 2 + [hops] * 2 + [PARTS * n_z] * 4 + [hops] * 2 + [turns] * 3
    planes = pl.pallas_call(
        functools.partial(spectrum_kernel, n_y, n_z, zl),
        out_shape=jax.ShapeDtypeStruct((LH, PARTS, n_y, rows, tile), F32),
        in_specs=[pl.BlockSpec(memory_space=pl.ANY)] * len(operands),
        out_specs=pl.BlockSpec(memory_space=pl.ANY),
        scratch_shapes=[
            pltpu.VMEM(flat.shape, BF),
            pltpu.VMEM(x_rows.shape, BF),
            pltpu.VMEM((2, my_rows, 2 * y_rows.shape[3]), BF),
            pltpu.VMEM((2,) + y_back.shape[1:], BF),
            pltpu.VMEM(z_rows.shape, BF),
            pltpu.VMEM(z_back.shape, BF),
            pltpu.VMEM(weight.shape, BF),
            pltpu.VMEM((PARTS, n_y, rows, lanes), F32),
            pltpu.VMEM((PARTS, n_ring, rows, lanes), F32),
            pltpu.VMEM((PARTS, 2, reach, my_rows, tile), F32),
            pltpu.VMEM((PARTS, 2, reach, my_rows, tile), F32),
            pltpu.VMEM((PARTS, modes, part, tile), F32),
            pltpu.VMEM((PARTS, n_z, part, tile), F32),
            pltpu.VMEM((PARTS, n_z, part, tile), F32),
            pltpu.VMEM((PARTS, modes, part, tile), F32),
            pltpu.VMEM((PARTS, 2, reach, modes, part, tile), F32),
            pltpu.VMEM((PARTS, n_ring, LH, rows, tile), F32),
            pltpu.VMEM((PARTS, n_ring, LH, rows, tile), F32),
        ]
        + [pltpu.SemaphoreType.DMA((n,)) for n in sems],
        compiler_params=pltpu.CompilerParams(
            collective_id=0, has_side_effects=True, vmem_limit_bytes=62 * MIB
        ),
        name="spectrum",
    )(*operands)

    step = 8
    count = PARTS * n_y * 2 * kp
    block = pl.BlockSpec((c, step * zl, nx), lambda i: (0, i, 0))
    out = pl.pallas_call(
        functools.partial(field_kernel, zl),
        grid=(yl // step,),
        in_specs=[
            pl.BlockSpec((LH, count, step, tile), lambda i: (0, 0, i, 0)),
            block,
            whole(bypass_weight.shape),
            whole(bias.shape),
            whole(th.shape),
            whole(tl.shape),
        ],
        out_specs=block,
        out_shape=jax.ShapeDtypeStruct(flat.shape, BF),
        scratch_shapes=[pltpu.VMEM((lanes, lanes), BF), pltpu.VMEM((lanes, nx), F32)],
        compiler_params=pltpu.CompilerParams(vmem_limit_bytes=62 * MIB),
        name="field",
    )(planes.reshape(LH, count, yl, tile), flat, bypass_weight, bias, jnp.asarray(th), jnp.asarray(tl))
    return out.reshape(features.shape)


def solution(mesh):
    n_y, n_z = mesh.shape["py"], mesh.shape["pz"]

    def run(features, spectral_weight, bypass_weight, bias_vector):
        _, ny, nz, nx = features.shape
        _, mx, my, mz, _ = spectral_weight.shape
        tables = make_tables(nx, ny, nz, mx, my, mz, n_y, n_z)
        return jax.shard_map(
            functools.partial(per_device, tables, n_y, n_z),
            mesh=mesh,
            in_specs=(P(None, "py", "pz", None), P(None, "py", "pz", None, None), P(), P()),
            out_specs=P(None, "py", "pz", None),
            check_vma=False,
        )(features, spectral_weight, bypass_weight, bias_vector)

    return run
```

time: 107 us -> 102 us (0.953)
  Pallas kernels: 106 us -> 102 us
    pallas_call x1, Pallas kernels: 101 us -> 95.5 us  [per_device(): pl.pallas_call(functools.partial(spectrum_kernel, n_y, n_z, zl), out_shap...]
    pallas_call x1, Pallas kernels: 5.34 us -> 6.6 us  [per_device(): pl.pallas_call(functools.partial(field_kernel, zl), grid=(yl // step,), i...]
where the time goes in v5:
time: 102 us
  Pallas kernels  102 us (100%)
    pallas_call x1, Pallas kernels, per_device(): pl.pallas_call(functools.partial(spectrum_kernel, n_y, n_z, zl), out_shap...  95.5 us
    pallas_call x1, Pallas kernels, per_device(): pl.pallas_call(functools.partial(field_kernel, zl), grid=(yl // step,), i...  6.6 us

profile of v5, /device:TPU:6, one launch (start us, length us, event | category | flops | bytes accessed | tf_op | source)
XLA Modules:
  0.0 102.1 jit_solution(4381817242967593455)
XLA Ops:
  0.0 95.5 %spectrum.1 = f32[2,2,16,64,128]{4,3,2,1,0:T(8,128)} custom-call(bf16[32,128,256]{2,1,0:T(8,128)(2,1)} %bitcast.5, bf16[2,256,512]{2,1,0:T(8,128)(2,1)} %constant.14.clone.refs_1_, bf16[16,2,256,128]{3,2,1,0:T(8,128)(2,1)} %constant.15.clone.refs_2_, bf16[16,2,128,256]{3,2,1,0:T(8,128)(2,1)} %constant.16.clone.refs_3_, ...), custom_call_target="tpu_custom_call" | custom-call | tf_op jit(solution)/shard_map/spectrum/pallas_call | solution.py:538
  95.5 6.6 %field.1 = bf16[32,128,256]{2,1,0:T(8,128)(2,1)} custom-call(f32[2,128,16,128]{3,2,1,0:T(8,128)} %bitcast.7, bf16[32,128,256]{2,1,0:T(8,128)(2,1)} %bitcast.6, bf16[32,32]{1,0:T(8,128)(2,1)} %w_ref.1, f32[1,32]{1,0:T(1,128)} %bitcast.9, bf16[256,256]{1,0:T(8,128)(2,1)} %constant.19.clone.th_ref, bf16[128,256]{1,0:T(8,128)(2,1)} %constant.20.clone.tl_ref), custom_call_target="tpu_custom_call" | custom-call | tf_op jit(solution)/shard_map/field/pallas_call | solution.py:573

commit v6 on v5

--- a/solution.py
+++ b/solution.py
@@ -15,6 +15,7 @@
 F32 = jnp.float32
 MIB = 1 << 20
 PARTS = 2
+STRIP = 8
 LH = 2
 GROUP = 4
 
@@ -50,8 +51,7 @@
     kp = k // PARTS
     eye, pairs = np.eye(kp), np.eye(2)
     xf = np.stack([np.cos(angle) * norm, -np.sin(angle) * norm], 1)
-    xf = xf.reshape(py, PARTS, kp, 2, nx)
-    xf = np.einsum("dtkpx,yw->tdykpwx", xf, pairs).reshape(PARTS, py * 4 * kp, 2 * nx)
+    xf = xf.reshape(py, PARTS, kp, 2, nx).swapaxes(0, 1).reshape(2 * mx, nx)
     weight = np.where(np.arange(mx) == 0, 1.0, 2.0)[:, None] * norm
     xi = np.stack([np.cos(angle) * weight, -np.sin(angle) * weight], 1)
     xi = xi.reshape(py, PARTS, kp, 2, nx).swapaxes(0, 1).reshape(2 * mx, nx)
@@ -60,7 +60,8 @@
     yf = np.einsum("pqdyj,kl,hg->djhkqgylp", yf, eye, pairs)
     yf = yf.reshape(py, my * 4 * kp, yl * 4 * kp)
     yi = pair(centred(my), np.arange(ny), ny, 1.0)[..., order].reshape(2, 2, py, yl, my)
-    yi = np.einsum("qrdyj,kl,hg->dhkryjglq", yi, eye, pairs)
+    yi = yi.reshape(2, 2, py, yl // STRIP, STRIP, my)
+    yi = np.einsum("qrdwyj,kl,hg->dwhkryjglq", yi, eye, pairs)
     yi = yi.reshape(py, yl * 4 * kp, my * 4 * kp)
     zf = pair(centred(mz), np.arange(nz), nz, -1.0).reshape(2, 2, pz, zl, mz)
     zf = np.einsum("pqszm->zqmps", zf).reshape(zl, 2 * mz, 2 * pz)
@@ -87,21 +88,28 @@
     return dot(ah, bh) + dot(al, bh) + dot(ah, bl)
 
 
-def x_forward(zl, field, table, out, t, first, last):
+def x_forward(zl, field, table, out, first, last):
     length = field.shape[2]
+    parts, owners, two, _, lanes = out.shape
 
     def step(i, carry):
         block = field[:, pl.ds(pl.multiple_of(i * 2 * zl, 2 * zl), 2 * zl), :].astype(F32)
-        both = None
+        planes = []
         for y in range(2):
             plane = block[:, y * zl : (y + 1) * zl, :].reshape(-1, length).astype(BF)
-            term = dot(table[t, :, y * length : (y + 1) * length], plane, ((1,), (1,)))
-            both = term if both is None else both + term
-        half = both.shape[0] // 2
-        rows = half // out.shape[1]
-        out[t, :, pl.ds(pl.multiple_of(i * rows, rows), rows), :] = (
-            both[:half] + both[half:]
-        ).reshape(out.shape[1], rows, out.shape[3])
+            both = dot(table[...], plane, ((1,), (1,)))
+            half = both.shape[0] // 2
+            planes.append((both[:half] + both[half:]).reshape(parts * owners, -1, lanes))
+        first_y, second_y = planes
+        rows = first_y.shape[1]
+        upper = lax.broadcasted_iota(jnp.int32, (1, rows, 1), 1) < rows // 2
+        turned = lambda v: pltpu.roll(v, rows // 2, 1)
+        even = jnp.where(upper, first_y, turned(second_y))
+        odd = jnp.where(upper, turned(first_y), second_y)
+        at = pl.ds(pl.multiple_of(i * rows, rows), rows)
+        for t in range(parts):
+            out[t, :, 0, at, :] = even[t * owners : (t + 1) * owners]
+            out[t, :, 1, at, :] = odd[t * owners : (t + 1) * owners]
         return carry
 
     lax.fori_loop(first, last, step, 0)
@@ -211,6 +219,27 @@
         load(f_hbm.at[:, pl.ds(i * rows, rows), :], f.at[:, pl.ds(i * rows, rows), :])
         for i in range(pieces)
     ]
+    lax.fori_loop(1, n_z, greet, 0)
+
+    reach = n_ring // 2
+    offsets = [reach] + [o * s for o in range(reach - 1, 0, -1) for s in (1, -1)] + [0]
+
+    def swap(h, i):
+        at = (z + offsets[i] + n_ring) % n_ring
+        return pltpu.make_async_remote_copy(
+            src_ref=a.at[h, half_py(other, at) // 2, at % 2],
+            dst_ref=theirs.at[h, at],
+            send_sem=swap_s.at[h * n_ring + i],
+            recv_sem=swap_r.at[h * n_ring + i],
+            device_id=partner,
+            device_id_type=MESH,
+        )
+
+    table_x.wait()
+    turns = f.shape[1] // (2 * zl) // pieces
+    for i in range(pieces):
+        fields[i].wait()
+        x_forward(zl, f, xt, a, i * turns, (i + 1) * turns)
     depth = yt_hbm.shape[3]
     table_y = [
         load(yt_hbm.at[half_py(s, z)], yt.at[:, :, pl.ds(i * depth, depth)])
@@ -218,31 +247,8 @@
     ]
     table_z = [load(zf_hbm, zf), load(w_hbm, w), load(zi_hbm, zi)]
     table_i = [load(yi_hbm.at[half_py(s, z)], yi.at[i]) for i, s in enumerate((side, other))]
-    lax.fori_loop(1, n_z, greet, 0)
-
-    reach = n_ring // 2
-    offsets = [reach] + [o * s for o in range(reach - 1, 0, -1) for s in (1, -1)] + [0]
-
-    def swap(h, i):
-        at = (z + offsets[i] + n_ring) % n_ring
-        return pltpu.make_async_remote_copy(
-            src_ref=a.at[h, half_py(other, at)],
-            dst_ref=theirs.at[h, at],
-            send_sem=swap_s.at[h * n_ring + i],
-            recv_sem=swap_r.at[h * n_ring + i],
-            device_id=partner,
-            device_id_type=MESH,
-        )
-
-    table_x.wait()
-    turns = f.shape[1] // (2 * zl) // pieces
+    pl.semaphore_wait(barrier, n_z + 2)
     for h in range(PARTS):
-        for i in range(pieces):
-            if h == 0:
-                fields[i].wait()
-            x_forward(zl, f, xt, a, h, i * turns, (i + 1) * turns)
-        if h == 0:
-            pl.semaphore_wait(barrier, n_z + 2)
         for i in range(n_ring):
             swap(h, i).start()
     for copy in table_y:
@@ -251,7 +257,7 @@
     def partial(h, i):
         at = (z + offsets[i] + n_ring) % n_ring
         swap(h, i).wait_recv()
-        rows = (a[h, half_py(side, at)], theirs[h, at])
+        rows = (a[h, half_py(side, at) // 2, at % 2], theirs[h, at])
         tile = summing.shape[4]
         block = jnp.concatenate(
             [r[:, i * tile : (i + 1) * tile] for r in rows for i in range(LH)], axis=0
@@ -293,6 +299,7 @@
 
     per = n_z // GROUP
     y_chip, place = column // GROUP, column % GROUP
+    far_first = lambda i: (y_chip + per // 2 + (i + 1) // 2 * (1 - i % 2 * 2) + per) % per
     slot = place * per + y_chip
 
     def to_owner(h, source, owner, target):
@@ -315,7 +322,7 @@
             total[h, g * per : (g + 1) * per] = value.reshape((per,) + total.shape[2:])
 
             def send(i, carry):
-                chip = (y_chip + i) % per
+                chip = far_first(i)
                 owner = chip * GROUP + g
 
                 @pl.when(owner != column)
@@ -367,7 +374,7 @@
                         ]
 
             def send_back(i, carry):
-                chip = (y_chip + i) % per
+                chip = far_first(i)
                 peer = chip * GROUP + g
 
                 @pl.when(peer != column)
@@ -406,7 +413,7 @@
     def turn(h, i, owner):
         return pltpu.make_async_remote_copy(
             src_ref=leaving.at[h, i],
-            dst_ref=r_hbm.at[:, h, owner],
+            dst_ref=r_hbm.at[:, :, h, owner],
             send_sem=turn_s.at[h * n_ring + i],
             recv_sem=turn_r.at[h * n_ring + i],
             device_id=partner,
@@ -415,7 +422,7 @@
 
     def keep(h, i, owner):
         return pltpu.make_async_copy(
-            keeping.at[h, i], r_hbm.at[:, h, owner], keep_s.at[h * n_ring + i]
+            keeping.at[h, i], r_hbm.at[:, :, h, owner], keep_s.at[h * n_ring + i]
         )
 
     def spread(h, i, offset, block):
@@ -465,14 +472,15 @@
     spread(0, 0, 0, back[0])
     collect(1)
     mix_and_return(1)
-    for step in range(1, reach):
+    for step in range(1, reach - 1):
         pass_on(0, step)
         spread_pair(0, step)
-    pass_on(0, reach)
     end_back(1)
     send_own(1)
-    spread_pair(0, reach)
     spread(1, 0, 0, back[1])
+    for step in range(reach - 1, reach + 1):
+        pass_on(0, step)
+        spread_pair(0, step)
     for step in range(1, reach + 1):
         pass_on(1, step)
         spread_pair(1, step)
@@ -498,12 +506,21 @@
         mix[...] = rows_mix
         shift[...] = jnp.broadcast_to(rows_bias, shift.shape)
 
-    block = f_ref[...].astype(F32)
-    for y in range(f_ref.shape[1] // zl):
-        plane = block[:, y * zl : (y + 1) * zl, :].reshape(-1, block.shape[2]).astype(BF)
-        values = jnp.concatenate([r_ref[i, :, y, :] for i in range(LH)], axis=1)
-        made = field_rows(zl, values, plane, mix[...], shift[...], th_ref[...], tl_ref[...])
-        o_ref[:, y * zl : (y + 1) * zl, :] = made.astype(BF)
+    def part(first):
+        block = f_ref[...].astype(F32)
+        for y in range(f_ref.shape[1] // zl):
+            plane = block[:, y * zl : (y + 1) * zl, :].reshape(-1, block.shape[2]).astype(BF)
+            values = jnp.concatenate([r_ref[0, i, :, first + y, :] for i in range(LH)], axis=1)
+            made = field_rows(zl, values, plane, mix[...], shift[...], th_ref[...], tl_ref[...])
+            o_ref[:, y * zl : (y + 1) * zl, :] = made.astype(BF)
+
+    @pl.when(pl.program_id(0) % 2 == 0)
+    def _():
+        part(0)
+
+    @pl.when(pl.program_id(0) % 2 == 1)
+    def _():
+        part(STRIP // 2)
 
 
 def whole(shape):
@@ -520,7 +537,7 @@
     rows = yl * 2 * kp
     part = LH * 2 * kp
     flat = features.reshape(c, yl * zl, nx)
-    x_rows = split(xf, 1).reshape(PARTS, -1, 2 * nx)
+    x_rows = split(xf).reshape(-1, nx)
     y_rows, y_back = split(yf, 1), split(yi, 1)
     z_rows, z_back = thrice(zf), thrice(zi)
     high, tl = split(xi)
@@ -531,13 +548,14 @@
     modes = my_rows // part
     n_ring = n_y // 2
     reach = n_ring // 2
+    strips = yl // STRIP
     operands = [flat] + [jnp.asarray(t) for t in (x_rows, y_rows, y_back, z_rows, z_back)] + [weight]
     hops = PARTS * 2 * reach * GROUP
     turns = PARTS * n_ring
     sems = [16] + [turns] * 2 + [hops] * 2 + [PARTS * n_z] * 4 + [hops] * 2 + [turns] * 3
     planes = pl.pallas_call(
         functools.partial(spectrum_kernel, n_y, n_z, zl),
-        out_shape=jax.ShapeDtypeStruct((LH, PARTS, n_y, rows, tile), F32),
+        out_shape=jax.ShapeDtypeStruct((strips, LH, PARTS, n_y, rows // strips, tile), F32),
         in_specs=[pl.BlockSpec(memory_space=pl.ANY)] * len(operands),
         out_specs=pl.BlockSpec(memory_space=pl.ANY),
         scratch_shapes=[
@@ -548,7 +566,7 @@
             pltpu.VMEM(z_rows.shape, BF),
             pltpu.VMEM(z_back.shape, BF),
             pltpu.VMEM(weight.shape, BF),
-            pltpu.VMEM((PARTS, n_y, rows, lanes), F32),
+            pltpu.VMEM((PARTS, n_y // 2, 2, rows, lanes), F32),
             pltpu.VMEM((PARTS, n_ring, rows, lanes), F32),
             pltpu.VMEM((PARTS, 2, reach, my_rows, tile), F32),
             pltpu.VMEM((PARTS, 2, reach, my_rows, tile), F32),
@@ -557,8 +575,8 @@
             pltpu.VMEM((PARTS, n_z, part, tile), F32),
             pltpu.VMEM((PARTS, modes, part, tile), F32),
             pltpu.VMEM((PARTS, 2, reach, modes, part, tile), F32),
-            pltpu.VMEM((PARTS, n_ring, LH, rows, tile), F32),
-            pltpu.VMEM((PARTS, n_ring, LH, rows, tile), F32),
+            pltpu.VMEM((PARTS, n_ring, strips, LH, rows // strips, tile), F32),
+            pltpu.VMEM((PARTS, n_ring, strips, LH, rows // strips, tile), F32),
         ]
         + [pltpu.SemaphoreType.DMA((n,)) for n in sems],
         compiler_params=pltpu.CompilerParams(
@@ -567,14 +585,14 @@
         name="spectrum",
     )(*operands)
 
-    step = 8
+    step = STRIP // 2
     count = PARTS * n_y * 2 * kp
     block = pl.BlockSpec((c, step * zl, nx), lambda i: (0, i, 0))
     out = pl.pallas_call(
         functools.partial(field_kernel, zl),
         grid=(yl // step,),
         in_specs=[
-            pl.BlockSpec((LH, count, step, tile), lambda i: (0, 0, i, 0)),
+            pl.BlockSpec((1, LH, count, STRIP, tile), lambda i: (i // 2, 0, 0, 0, 0)),
             block,
             whole(bypass_weight.shape),
             whole(bias.shape),
@@ -586,7 +604,7 @@
         scratch_shapes=[pltpu.VMEM((lanes, lanes), BF), pltpu.VMEM((lanes, nx), F32)],
         compiler_params=pltpu.CompilerParams(vmem_limit_bytes=62 * MIB),
         name="field",
-    )(planes.reshape(LH, count, yl, tile), flat, bypass_weight, bias, jnp.asarray(th), jnp.asarray(tl))
+    )(planes.reshape(strips, LH, count, STRIP, tile), flat, bypass_weight, bias, jnp.asarray(th), jnp.asarray(tl))
     return out.reshape(features.shape)
 
 

time: 102 us -> 100 us (0.980)
  Pallas kernels: 102 us -> 100 us
    pallas_call x1, Pallas kernels: 95.5 us -> 92.8 us  [per_device(): pl.pallas_call(functools.partial(spectrum_kernel, n_y, n_z, zl), out_shap...]
where the time goes in v6:
time: 100 us
  Pallas kernels  100 us (100%)
    pallas_call x1, Pallas kernels, per_device(): pl.pallas_call(functools.partial(spectrum_kernel, n_y, n_z, zl), out_shap...  92.8 us
    pallas_call x1, Pallas kernels, per_device(): pl.pallas_call(functools.partial(field_kernel, zl), grid=(yl // step,), i...  7.21 us

profile of v6, /device:TPU:6, one launch (start us, length us, event | category | flops | bytes accessed | tf_op | source)
XLA Modules:
  0.0 100.0 jit_solution(15952210088918290199)
XLA Ops:
  0.0 92.8 %spectrum.1 = f32[2,2,2,16,32,128]{5,4,3,2,1,0:T(8,128)} custom-call(bf16[32,128,256]{2,1,0:T(8,128)(2,1)} %bitcast.5, bf16[256,256]{1,0:T(8,128)(2,1)} %constant.14.clone.refs_1_, bf16[16,2,256,128]{3,2,1,0:T(8,128)(2,1)} %constant.15.clone.refs_2_, bf16[16,2,128,256]{3,2,1,0:T(8,128)(2,1)} %constant.16.clone.refs_3_, ...), custom_call_target="tpu_custom_call" | custom-call | tf_op jit(solution)/shard_map/spectrum/pallas_call | solution.py:556
  92.8 7.2 %field.1 = bf16[32,128,256]{2,1,0:T(8,128)(2,1)} custom-call(f32[2,2,128,8,128]{4,3,2,1,0:T(8,128)} %bitcast.7, bf16[32,128,256]{2,1,0:T(8,128)(2,1)} %bitcast.6, bf16[32,32]{1,0:T(8,128)(2,1)} %w_ref.1, f32[1,32]{1,0:T(1,128)} %bitcast.9, bf16[256,256]{1,0:T(8,128)(2,1)} %constant.19.clone.th_ref, bf16[128,256]{1,0:T(8,128)(2,1)} %constant.20.clone.tl_ref), custom_call_target="tpu_custom_call" | custom-call | tf_op jit(solution)/shard_map/field/pallas_call | solution.py:591

commit v7 on v6

--- a/solution.py
+++ b/solution.py
@@ -458,29 +458,31 @@
         move_on(0, step)
     set_out(1)
     arrive(0)
-    for step in range(1, reach):
+    for step in range(1, reach - 1):
         move_on(1, step)
     for copy in table_z:
         copy.wait()
     collect(0)
     mix_and_return(0)
+    move_on(1, reach - 1)
     arrive(1)
     for copy in table_i:
         copy.wait()
     end_back(0)
     send_own(0)
     spread(0, 0, 0, back[0])
+    pass_on(0, 1)
+    spread_pair(0, 1)
     collect(1)
     mix_and_return(1)
-    for step in range(1, reach - 1):
+    for step in range(2, reach):
         pass_on(0, step)
         spread_pair(0, step)
     end_back(1)
     send_own(1)
     spread(1, 0, 0, back[1])
-    for step in range(reach - 1, reach + 1):
-        pass_on(0, step)
-        spread_pair(0, step)
+    pass_on(0, reach)
+    spread_pair(0, reach)
     for step in range(1, reach + 1):
         pass_on(1, step)
         spread_pair(1, step)
@@ -499,32 +501,37 @@
                         relay(h, way, step, g).wait_send()
 
 
-def field_kernel(zl, r_ref, f_ref, w_ref, b_ref, th_ref, tl_ref, o_ref, mix, shift):
-    @pl.when(pl.program_id(0) == 0)
-    def _():
-        rows_mix, rows_bias = bypass_rows(zl, w_ref, b_ref)
-        mix[...] = rows_mix
-        shift[...] = jnp.broadcast_to(rows_bias, shift.shape)
-
-    def part(first):
-        block = f_ref[...].astype(F32)
-        for y in range(f_ref.shape[1] // zl):
+def field_kernel(
+    zl, r_hbm, f_hbm, w_ref, b_ref, th_ref, tl_ref, o_hbm, r, f, o, mix, shift, r_sem, f_sem, o_sem
+):
+    strips, pieces = r.shape[0], 4
+    rows = f.shape[1] // pieces
+    at = lambda i: (slice(None), pl.ds(i * rows, rows), slice(None))
+    strip = lambda i: pltpu.make_async_copy(r_hbm.at[i], r.at[i], r_sem.at[i])
+    fetch = lambda i: pltpu.make_async_copy(f_hbm.at[at(i)], f.at[at(i)], f_sem.at[i])
+    store = lambda i: pltpu.make_async_copy(o.at[at(i)], o_hbm.at[at(i)], o_sem.at[i])
+    each = pieces // strips
+    for i in range(strips):
+        strip(i).start()
+        for j in range(each):
+            fetch(i * each + j).start()
+    rows_mix, rows_bias = bypass_rows(zl, w_ref, b_ref)
+    mix[...] = rows_mix
+    shift[...] = jnp.broadcast_to(rows_bias, shift.shape)
+    for i in range(pieces):
+        if i % each == 0:
+            strip(i // each).wait()
+        fetch(i).wait()
+        block = f[:, i * rows : (i + 1) * rows, :].astype(F32)
+        for y in range(rows // zl):
             plane = block[:, y * zl : (y + 1) * zl, :].reshape(-1, block.shape[2]).astype(BF)
-            values = jnp.concatenate([r_ref[0, i, :, first + y, :] for i in range(LH)], axis=1)
+            within = i % each * (rows // zl) + y
+            values = jnp.concatenate([r[i // each, h, :, within, :] for h in range(LH)], axis=1)
             made = field_rows(zl, values, plane, mix[...], shift[...], th_ref[...], tl_ref[...])
-            o_ref[:, y * zl : (y + 1) * zl, :] = made.astype(BF)
-
-    @pl.when(pl.program_id(0) % 2 == 0)
-    def _():
-        part(0)
-
-    @pl.when(pl.program_id(0) % 2 == 1)
-    def _():
-        part(STRIP // 2)
-
-
-def whole(shape):
-    return pl.BlockSpec(shape, lambda i: (0,) * len(shape))
+            o[:, i * rows + y * zl : i * rows + (y + 1) * zl, :] = made.astype(BF)
+        store(i).start()
+    for i in range(pieces):
+        store(i).wait()
 
 
 def per_device(tables, n_y, n_z, features, spectral_weight, bypass_weight, bias_vector):
@@ -585,26 +592,32 @@
         name="spectrum",
     )(*operands)
 
-    step = STRIP // 2
     count = PARTS * n_y * 2 * kp
-    block = pl.BlockSpec((c, step * zl, nx), lambda i: (0, i, 0))
     out = pl.pallas_call(
         functools.partial(field_kernel, zl),
-        grid=(yl // step,),
-        in_specs=[
-            pl.BlockSpec((1, LH, count, STRIP, tile), lambda i: (i // 2, 0, 0, 0, 0)),
-            block,
-            whole(bypass_weight.shape),
-            whole(bias.shape),
-            whole(th.shape),
-            whole(tl.shape),
+        in_specs=[pl.BlockSpec(memory_space=pl.ANY)] * 2 + [pl.BlockSpec(memory_space=pltpu.VMEM)] * 4,
+        out_specs=pl.BlockSpec(memory_space=pl.ANY),
+        out_shape=jax.ShapeDtypeStruct(flat.shape, BF),
+        scratch_shapes=[
+            pltpu.VMEM((strips, LH, count, STRIP, tile), F32),
+            pltpu.VMEM(flat.shape, BF),
+            pltpu.VMEM(flat.shape, BF),
+            pltpu.VMEM((lanes, lanes), BF),
+            pltpu.VMEM((lanes, nx), F32),
+            pltpu.SemaphoreType.DMA((strips,)),
+            pltpu.SemaphoreType.DMA((4,)),
+            pltpu.SemaphoreType.DMA((4,)),
         ],
-        out_specs=block,
-        out_shape=jax.ShapeDtypeStruct(flat.shape, BF),
-        scratch_shapes=[pltpu.VMEM((lanes, lanes), BF), pltpu.VMEM((lanes, nx), F32)],
         compiler_params=pltpu.CompilerParams(vmem_limit_bytes=62 * MIB),
         name="field",
-    )(planes.reshape(strips, LH, count, STRIP, tile), flat, bypass_weight, bias, jnp.asarray(th), jnp.asarray(tl))
+    )(
+        planes.reshape(strips, LH, count, STRIP, tile),
+        flat,
+        bypass_weight,
+        bias,
+        jnp.asarray(th),
+        jnp.asarray(tl),
+    )
     return out.reshape(features.shape)
 
 

time: 100 us -> 99.9 us (level)
  Pallas kernels: 100 us -> 98.7 us
    pallas_call x1, Pallas kernels: 92.8 us -> 91.2 us  [per_device(): pl.pallas_call(functools.partial(spectrum_kernel, n_y, n_z, zl), out_shap...]
where the time goes in v7:
time: 99.9 us; the launch traced here: 98.9 us
  Pallas kernels  98.7 us (99%)
    pallas_call x1, Pallas kernels, per_device(): pl.pallas_call(functools.partial(spectrum_kernel, n_y, n_z, zl), out_shap...  91.2 us
    pallas_call x1, Pallas kernels, per_device(): pl.pallas_call(functools.partial(field_kernel, zl), in_specs=[pl.BlockSpe...  7.5 us

profile of v7, /device:TPU:6, one launch (start us, length us, event | category | flops | bytes accessed | tf_op | source)
XLA Modules:
  0.0 98.9 jit_solution(2232259671441751641)
XLA Ops:
  0.0 91.2 %spectrum.1 = f32[2,2,2,16,32,128]{5,4,3,2,1,0:T(8,128)} custom-call(bf16[32,128,256]{2,1,0:T(8,128)(2,1)} %bitcast.5, bf16[256,256]{1,0:T(8,128)(2,1)} %constant.14.clone.refs_1_, bf16[16,2,256,128]{3,2,1,0:T(8,128)(2,1)} %constant.15.clone.refs_2_, bf16[16,2,128,256]{3,2,1,0:T(8,128)(2,1)} %constant.16.clone.refs_3_, ...), custom_call_target="tpu_custom_call" | custom-call | tf_op jit(solution)/shard_map/spectrum/pallas_call | solution.py:563
  91.2 7.5 %field.1 = bf16[32,128,256]{2,1,0:T(8,128)(2,1)} custom-call(f32[2,2,128,8,128]{4,3,2,1,0:T(8,128)} %bitcast.7, bf16[32,128,256]{2,1,0:T(8,128)(2,1)} %bitcast.6, bf16[32,32]{1,0:T(8,128)(2,1)} %w_ref.1, f32[1,32]{1,0:T(1,128)} %bitcast.9, bf16[256,256]{1,0:T(8,128)(2,1)} %constant.19.clone.th_ref, bf16[128,256]{1,0:T(8,128)(2,1)} %constant.20.clone.tl_ref), custom_call_target="tpu_custom_call" | custom-call | tf_op jit(solution)/shard_map/field/pallas_call | solution.py:596

commit v8 on v6

--- a/solution.py
+++ b/solution.py
@@ -15,7 +15,7 @@
 F32 = jnp.float32
 MIB = 1 << 20
 PARTS = 2
-STRIP = 8
+STRIP = 4
 LH = 2
 GROUP = 4
 
@@ -61,7 +61,7 @@
     yf = yf.reshape(py, my * 4 * kp, yl * 4 * kp)
     yi = pair(centred(my), np.arange(ny), ny, 1.0)[..., order].reshape(2, 2, py, yl, my)
     yi = yi.reshape(2, 2, py, yl // STRIP, STRIP, my)
-    yi = np.einsum("qrdwyj,kl,hg->dwhkryjglq", yi, eye, pairs)
+    yi = np.einsum("qrdwyj,kl,hg->dwhykrjglq", yi, eye, pairs)
     yi = yi.reshape(py, yl * 4 * kp, my * 4 * kp)
     zf = pair(centred(mz), np.arange(nz), nz, -1.0).reshape(2, 2, pz, zl, mz)
     zf = np.einsum("pqszm->zqmps", zf).reshape(zl, 2 * mz, 2 * pz)
@@ -170,14 +170,6 @@
     return jnp.where(a == b, full, 0.0).astype(BF), column
 
 
-def field_rows(zl, spectrum, plane, mix, column, th, tl):
-    high, low = halves(spectrum)
-    first = ((0,), (0,))
-    value = dot(jnp.concatenate([high, low], 0), th, first) + dot(high, tl, first)
-    value = value + dot(mix, plane) + column
-    return jax.nn.gelu(value).reshape(-1, zl, value.shape[1])
-
-
 def spectrum_kernel(n_y, n_z, zl, *refs):
     (
         f_hbm, xt_hbm, yt_hbm, yi_hbm, zf_hbm, zi_hbm, w_hbm, r_hbm,
@@ -224,22 +216,34 @@
     reach = n_ring // 2
     offsets = [reach] + [o * s for o in range(reach - 1, 0, -1) for s in (1, -1)] + [0]
 
-    def swap(h, i):
+    def swap(h, i, s):
         at = (z + offsets[i] + n_ring) % n_ring
+        half = theirs.shape[2] // 2
+        index = (h * n_ring + i) * 2 + s
         return pltpu.make_async_remote_copy(
-            src_ref=a.at[h, half_py(other, at) // 2, at % 2],
-            dst_ref=theirs.at[h, at],
-            send_sem=swap_s.at[h * n_ring + i],
-            recv_sem=swap_r.at[h * n_ring + i],
+            src_ref=a.at[h, half_py(other, at) // 2, at % 2, pl.ds(s * half, half)],
+            dst_ref=theirs.at[h, at, pl.ds(s * half, half)],
+            send_sem=swap_s.at[index],
+            recv_sem=swap_r.at[index],
             device_id=partner,
             device_id_type=MESH,
         )
 
     table_x.wait()
     turns = f.shape[1] // (2 * zl) // pieces
+    early = 2
     for i in range(pieces):
         fields[i].wait()
         x_forward(zl, f, xt, a, i * turns, (i + 1) * turns)
+        if i == pieces // 2 - 1:
+            pl.semaphore_wait(barrier, n_z + 2)
+            for j in range(early):
+                swap(0, j, 0).start()
+    for h in range(PARTS):
+        for i in range(n_ring):
+            for s in range(2):
+                if h > 0 or i >= early or s > 0:
+                    swap(h, i, s).start()
     depth = yt_hbm.shape[3]
     table_y = [
         load(yt_hbm.at[half_py(s, z)], yt.at[:, :, pl.ds(i * depth, depth)])
@@ -247,16 +251,13 @@
     ]
     table_z = [load(zf_hbm, zf), load(w_hbm, w), load(zi_hbm, zi)]
     table_i = [load(yi_hbm.at[half_py(s, z)], yi.at[i]) for i, s in enumerate((side, other))]
-    pl.semaphore_wait(barrier, n_z + 2)
-    for h in range(PARTS):
-        for i in range(n_ring):
-            swap(h, i).start()
     for copy in table_y:
         copy.wait()
 
     def partial(h, i):
         at = (z + offsets[i] + n_ring) % n_ring
-        swap(h, i).wait_recv()
+        for s in range(2):
+            swap(h, i, s).wait_recv()
         rows = (a[h, half_py(side, at) // 2, at % 2], theirs[h, at])
         tile = summing.shape[4]
         block = jnp.concatenate(
@@ -458,36 +459,39 @@
         move_on(0, step)
     set_out(1)
     arrive(0)
-    for step in range(1, reach):
+    for step in range(1, reach - 1):
         move_on(1, step)
     for copy in table_z:
         copy.wait()
     collect(0)
     mix_and_return(0)
+    move_on(1, reach - 1)
     arrive(1)
     for copy in table_i:
         copy.wait()
     end_back(0)
     send_own(0)
     spread(0, 0, 0, back[0])
+    pass_on(0, 1)
+    spread_pair(0, 1)
     collect(1)
     mix_and_return(1)
-    for step in range(1, reach - 1):
+    for step in range(2, reach):
         pass_on(0, step)
         spread_pair(0, step)
     end_back(1)
     send_own(1)
     spread(1, 0, 0, back[1])
-    for step in range(reach - 1, reach + 1):
-        pass_on(0, step)
-        spread_pair(0, step)
+    pass_on(0, reach)
+    spread_pair(0, reach)
     for step in range(1, reach + 1):
         pass_on(1, step)
         spread_pair(1, step)
 
     for h in range(PARTS):
         for i in range(n_ring):
-            swap(h, i).wait_send()
+            for s in range(2):
+                swap(h, i, s).wait_send()
             keep(h, i, here).wait()
             turn(h, i, here).wait()
         for step in range(reach):
@@ -506,21 +510,21 @@
         mix[...] = rows_mix
         shift[...] = jnp.broadcast_to(rows_bias, shift.shape)
 
-    def part(first):
-        block = f_ref[...].astype(F32)
-        for y in range(f_ref.shape[1] // zl):
+    block = f_ref[...].astype(F32)
+    rows = r_ref.shape[3] * 2 // STRIP
+    for pair in range(STRIP // 2):
+        tiles = [
+            r_ref[0, h, :, pair * rows : (pair + 1) * rows, :].reshape(-1, r_ref.shape[4])
+            for h in range(LH)
+        ]
+        high, low = halves(jnp.concatenate(tiles, axis=1).T)
+        for i in range(2):
+            y = pair * 2 + i
             plane = block[:, y * zl : (y + 1) * zl, :].reshape(-1, block.shape[2]).astype(BF)
-            values = jnp.concatenate([r_ref[0, i, :, first + y, :] for i in range(LH)], axis=1)
-            made = field_rows(zl, values, plane, mix[...], shift[...], th_ref[...], tl_ref[...])
-            o_ref[:, y * zl : (y + 1) * zl, :] = made.astype(BF)
-
-    @pl.when(pl.program_id(0) % 2 == 0)
-    def _():
-        part(0)
-
-    @pl.when(pl.program_id(0) % 2 == 1)
-    def _():
-        part(STRIP // 2)
+            value = dot(high, th_ref[i]) + dot(low, th_ref[i]) + dot(high, tl_ref[i])
+            value = value + dot(mix[...], plane) + shift[...]
+            out = jax.nn.gelu(value).reshape(block.shape[0], zl, block.shape[2])
+            o_ref[:, y * zl : (y + 1) * zl, :] = out.astype(BF)
 
 
 def whole(shape):
@@ -540,8 +544,8 @@
     x_rows = split(xf).reshape(-1, nx)
     y_rows, y_back = split(yf, 1), split(yi, 1)
     z_rows, z_back = thrice(zf), thrice(zi)
-    high, tl = split(xi)
-    th = np.concatenate([high, high], 0)
+    pair_rows = np.einsum("ekx,yw->weykx", xi.reshape(PARTS * n_y, -1, nx), np.eye(2))
+    th, tl = split(pair_rows.reshape(2, -1, nx))
     weight = spectral_weight.reshape(2, kl * mz, pairs)
     bias = bias_vector.reshape(1, c)
     my_rows = y_rows.shape[2]
@@ -552,7 +556,7 @@
     operands = [flat] + [jnp.asarray(t) for t in (x_rows, y_rows, y_back, z_rows, z_back)] + [weight]
     hops = PARTS * 2 * reach * GROUP
     turns = PARTS * n_ring
-    sems = [16] + [turns] * 2 + [hops] * 2 + [PARTS * n_z] * 4 + [hops] * 2 + [turns] * 3
+    sems = [16] + [turns * 2] * 2 + [hops] * 2 + [PARTS * n_z] * 4 + [hops] * 2 + [turns] * 3
     planes = pl.pallas_call(
         functools.partial(spectrum_kernel, n_y, n_z, zl),
         out_shape=jax.ShapeDtypeStruct((strips, LH, PARTS, n_y, rows // strips, tile), F32),
@@ -585,14 +589,13 @@
         name="spectrum",
     )(*operands)
 
-    step = STRIP // 2
-    count = PARTS * n_y * 2 * kp
-    block = pl.BlockSpec((c, step * zl, nx), lambda i: (0, i, 0))
+    block = pl.BlockSpec((c, STRIP * zl, nx), lambda i: (0, i, 0))
+    planes = planes.reshape(strips, LH, PARTS * n_y, rows // strips, tile)
     out = pl.pallas_call(
         functools.partial(field_kernel, zl),
-        grid=(yl // step,),
+        grid=(strips,),
         in_specs=[
-            pl.BlockSpec((1, LH, count, STRIP, tile), lambda i: (i // 2, 0, 0, 0, 0)),
+            pl.BlockSpec((1,) + planes.shape[1:], lambda i: (i, 0, 0, 0, 0)),
             block,
             whole(bypass_weight.shape),
             whole(bias.shape),
@@ -604,7 +607,7 @@
         scratch_shapes=[pltpu.VMEM((lanes, lanes), BF), pltpu.VMEM((lanes, nx), F32)],
         compiler_params=pltpu.CompilerParams(vmem_limit_bytes=62 * MIB),
         name="field",
-    )(planes.reshape(strips, LH, count, STRIP, tile), flat, bypass_weight, bias, jnp.asarray(th), jnp.asarray(tl))
+    )(planes, flat, bypass_weight, bias, jnp.asarray(th), jnp.asarray(tl))
     return out.reshape(features.shape)
 
 

time: 100 us -> 99.4 us (level)
  Pallas kernels: 100 us -> 98.9 us
where the time goes in v8:
time: 99.4 us; the launch traced here: 98.9 us
  Pallas kernels  98.9 us (99%)
    pallas_call x1, Pallas kernels, per_device(): pl.pallas_call(functools.partial(spectrum_kernel, n_y, n_z, zl), out_shap...  92 us
    pallas_call x1, Pallas kernels, per_device(): pl.pallas_call(functools.partial(field_kernel, zl), grid=(strips,), in_sp...  6.93 us

profile of v8, /device:TPU:6, one launch (start us, length us, event | category | flops | bytes accessed | tf_op | source)
XLA Modules:
  0.0 98.9 jit_solution(15620760741350023145)
XLA Ops:
  0.0 92.0 %spectrum.1 = f32[4,2,2,16,16,128]{5,4,3,2,1,0:T(8,128)} custom-call(bf16[32,128,256]{2,1,0:T(8,128)(2,1)} %bitcast.5, bf16[256,256]{1,0:T(8,128)(2,1)} %constant.14.clone.refs_1_, bf16[16,2,256,128]{3,2,1,0:T(8,128)(2,1)} %constant.15.clone.refs_2_, bf16[16,2,128,256]{3,2,1,0:T(8,128)(2,1)} %constant.16.clone.refs_3_, ...), custom_call_target="tpu_custom_call" | custom-call | tf_op jit(solution)/shard_map/spectrum/pallas_call | solution.py:560
  92.0 6.9 %field.1 = bf16[32,128,256]{2,1,0:T(8,128)(2,1)} custom-call(f32[4,2,32,16,128]{4,3,2,1,0:T(8,128)} %bitcast.7, bf16[32,128,256]{2,1,0:T(8,128)(2,1)} %bitcast.6, bf16[32,32]{1,0:T(8,128)(2,1)} %w_ref.1, f32[1,32]{1,0:T(1,128)} %bitcast.9, bf16[2,256,256]{2,1,0:T(8,128)(2,1)} %constant.19.clone.th_ref, bf16[2,256,256]{2,1,0:T(8,128)(2,1)} %constant.20.clone.tl_ref), custom_call_target="tpu_custom_call" | custom-call | tf_op jit(solution)/shard_map/field/pallas_call | solution.py:594

commit v9 on v8

--- a/solution.py
+++ b/solution.py
@@ -414,7 +414,7 @@
     def turn(h, i, owner):
         return pltpu.make_async_remote_copy(
             src_ref=leaving.at[h, i],
-            dst_ref=r_hbm.at[:, :, h, owner],
+            dst_ref=r_hbm.at[h, owner],
             send_sem=turn_s.at[h * n_ring + i],
             recv_sem=turn_r.at[h * n_ring + i],
             device_id=partner,
@@ -423,7 +423,7 @@
 
     def keep(h, i, owner):
         return pltpu.make_async_copy(
-            keeping.at[h, i], r_hbm.at[:, :, h, owner], keep_s.at[h * n_ring + i]
+            keeping.at[h, i], r_hbm.at[h, owner], keep_s.at[h * n_ring + i]
         )
 
     def spread(h, i, offset, block):
@@ -514,7 +514,7 @@
     rows = r_ref.shape[3] * 2 // STRIP
     for pair in range(STRIP // 2):
         tiles = [
-            r_ref[0, h, :, pair * rows : (pair + 1) * rows, :].reshape(-1, r_ref.shape[4])
+            r_ref[:, 0, h, pair * rows : (pair + 1) * rows, :].reshape(-1, r_ref.shape[4])
             for h in range(LH)
         ]
         high, low = halves(jnp.concatenate(tiles, axis=1).T)
@@ -559,7 +559,7 @@
     sems = [16] + [turns * 2] * 2 + [hops] * 2 + [PARTS * n_z] * 4 + [hops] * 2 + [turns] * 3
     planes = pl.pallas_call(
         functools.partial(spectrum_kernel, n_y, n_z, zl),
-        out_shape=jax.ShapeDtypeStruct((strips, LH, PARTS, n_y, rows // strips, tile), F32),
+        out_shape=jax.ShapeDtypeStruct((PARTS, n_y, strips, LH, rows // strips, tile), F32),
         in_specs=[pl.BlockSpec(memory_space=pl.ANY)] * len(operands),
         out_specs=pl.BlockSpec(memory_space=pl.ANY),
         scratch_shapes=[
@@ -590,12 +590,12 @@
     )(*operands)
 
     block = pl.BlockSpec((c, STRIP * zl, nx), lambda i: (0, i, 0))
-    planes = planes.reshape(strips, LH, PARTS * n_y, rows // strips, tile)
+    planes = planes.reshape(PARTS * n_y, strips, LH, rows // strips, tile)
     out = pl.pallas_call(
         functools.partial(field_kernel, zl),
         grid=(strips,),
         in_specs=[
-            pl.BlockSpec((1,) + planes.shape[1:], lambda i: (i, 0, 0, 0, 0)),
+            pl.BlockSpec((PARTS * n_y, 1) + planes.shape[2:], lambda i: (0, i, 0, 0, 0)),
             block,
             whole(bypass_weight.shape),
             whole(bias.shape),

time: 99.4 us -> 99.4 us (level)
  no operation moved by 1% of the time
where the time goes in v9:
time: 99.4 us; the launch traced here: 99 us
  Pallas kernels  98.9 us (99%)
    pallas_call x1, Pallas kernels, per_device(): pl.pallas_call(functools.partial(spectrum_kernel, n_y, n_z, zl), out_shap...  92 us
    pallas_call x1, Pallas kernels, per_device(): pl.pallas_call(functools.partial(field_kernel, zl), grid=(strips,), in_sp...  6.94 us

profile of v9, /device:TPU:6, one launch (start us, length us, event | category | flops | bytes accessed | tf_op | source)
XLA Modules:
  0.0 99.0 jit_solution(2051971524615514121)
XLA Ops:
  0.0 92.0 %spectrum.1 = f32[2,16,4,2,16,128]{5,4,3,2,1,0:T(8,128)} custom-call(bf16[32,128,256]{2,1,0:T(8,128)(2,1)} %bitcast.5, bf16[256,256]{1,0:T(8,128)(2,1)} %constant.14.clone.refs_1_, bf16[16,2,256,128]{3,2,1,0:T(8,128)(2,1)} %constant.15.clone.refs_2_, bf16[16,2,128,256]{3,2,1,0:T(8,128)(2,1)} %constant.16.clone.refs_3_, ...), custom_call_target="tpu_custom_call" | custom-call | tf_op jit(solution)/shard_map/spectrum/pallas_call | solution.py:560
  92.0 6.9 %field.1 = bf16[32,128,256]{2,1,0:T(8,128)(2,1)} custom-call(f32[32,4,2,16,128]{4,3,2,1,0:T(8,128)} %bitcast.7, bf16[32,128,256]{2,1,0:T(8,128)(2,1)} %bitcast.6, bf16[32,32]{1,0:T(8,128)(2,1)} %w_ref.1, f32[1,32]{1,0:T(1,128)} %bitcast.9, bf16[2,256,256]{2,1,0:T(8,128)(2,1)} %constant.19.clone.th_ref, bf16[2,256,256]{2,1,0:T(8,128)(2,1)} %constant.20.clone.tl_ref), custom_call_target="tpu_custom_call" | custom-call | tf_op jit(solution)/shard_map/field/pallas_call | solution.py:594

commit v10 on v9

--- a/solution.py
+++ b/solution.py
@@ -518,13 +518,15 @@
             for h in range(LH)
         ]
         high, low = halves(jnp.concatenate(tiles, axis=1).T)
+        made = []
         for i in range(2):
             y = pair * 2 + i
             plane = block[:, y * zl : (y + 1) * zl, :].reshape(-1, block.shape[2]).astype(BF)
             value = dot(high, th_ref[i]) + dot(low, th_ref[i]) + dot(high, tl_ref[i])
             value = value + dot(mix[...], plane) + shift[...]
-            out = jax.nn.gelu(value).reshape(block.shape[0], zl, block.shape[2])
-            o_ref[:, y * zl : (y + 1) * zl, :] = out.astype(BF)
+            made.append(jax.nn.gelu(value).reshape(block.shape[0], zl, block.shape[2]))
+        at = slice(pair * 2 * zl, (pair + 1) * 2 * zl)
+        o_ref[:, at, :] = jnp.concatenate(made, axis=1).astype(BF)
 
 
 def whole(shape):

time: 99.4 us -> 99.4 us (level)
  no operation moved by 1% of the time
where the time goes in v10:
time: 99.4 us; the launch traced here: 99 us
  Pallas kernels  98.9 us (99%)
    pallas_call x1, Pallas kernels, per_device(): pl.pallas_call(functools.partial(spectrum_kernel, n_y, n_z, zl), out_shap...  92 us
    pallas_call x1, Pallas kernels, per_device(): pl.pallas_call(functools.partial(field_kernel, zl), grid=(strips,), in_sp...  6.94 us

profile of v10, /device:TPU:6, one launch (start us, length us, event | category | flops | bytes accessed | tf_op | source)
XLA Modules:
  0.0 99.0 jit_solution(2051971524615514121)
XLA Ops:
  0.0 92.0 %spectrum.1 = f32[2,16,4,2,16,128]{5,4,3,2,1,0:T(8,128)} custom-call(bf16[32,128,256]{2,1,0:T(8,128)(2,1)} %bitcast.5, bf16[256,256]{1,0:T(8,128)(2,1)} %constant.14.clone.refs_1_, bf16[16,2,256,128]{3,2,1,0:T(8,128)(2,1)} %constant.15.clone.refs_2_, bf16[16,2,128,256]{3,2,1,0:T(8,128)(2,1)} %constant.16.clone.refs_3_, ...), custom_call_target="tpu_custom_call" | custom-call | tf_op jit(solution)/shard_map/spectrum/pallas_call | solution.py:562
  92.0 6.9 %field.1 = bf16[32,128,256]{2,1,0:T(8,128)(2,1)} custom-call(f32[32,4,2,16,128]{4,3,2,1,0:T(8,128)} %bitcast.7, bf16[32,128,256]{2,1,0:T(8,128)(2,1)} %bitcast.6, bf16[32,32]{1,0:T(8,128)(2,1)} %w_ref.1, f32[1,32]{1,0:T(1,128)} %bitcast.9, bf16[2,256,256]{2,1,0:T(8,128)(2,1)} %constant.19.clone.th_ref, bf16[2,256,256]{2,1,0:T(8,128)(2,1)} %constant.20.clone.tl_ref), custom_call_target="tpu_custom_call" | custom-call | tf_op jit(solution)/shard_map/field/pallas_call | solution.py:596
